TPU v7x, 512 devices: a whole 4x4x16 slice. The times are simulated.
512 devices in a mesh: wide: 64 (over x, z), narrow: 8 (over y, core).
Axes of the slice: x: 4, y: 4, z: 16, core: 2. Of those that a mesh axis runs over, the one named last changes fastest.
Arguments:
- table: bfloat16 [16384, 512], P('wide'), may hold values from -6 to 6
- item_owner: int32 [65536, 1], P(('wide', 'narrow')), may hold values from 0 to 63; in each aligned block of 128 rows (0 to 127, 128 to 255, ...) at most 8 rows name the same one
- item_row: int32 [65536], P(('wide', 'narrow')), may hold values from 0 to 255
- lengths: int32 [512, 6], P(('wide', 'narrow')), may hold values from 1 to 64, 128 in all within a row
- cotangent: bfloat16 [65536, 512], P(('wide', 'narrow')), may hold values from -24 to 24
- w_uvqk: bfloat16 [512, 2048], replicated, may hold values from -0.25 to 0.25
- w_out: bfloat16 [512, 512], replicated, may hold values from -0.25 to 0.25
Outputs:
- grad_table: float32 [16384, 512], P('wide')
- grad_uvqk: float32 [512, 2048], P('narrow', 'wide')
- grad_out: float32 [512, 512], P('narrow', 'wide')
Inputs may be any that keep to these rules, and one draw needn't show every extreme that they name: `item_owner`: among the actions of one block, at most 8 name the same owner, and some blocks reach 8. `lengths`: each row sums to 128 and its largest entry is 64.
All inputs are finite; a program needn't handle non-finite values.
Results may differ from a plain program's by a relative error of at most 0.024.
Values may be sent and summed in bfloat16 or wider, within the bound.
A program may use at most 64 MiB of HBM per device.

v0:
```python
import jax
import jax.numpy as jnp
from jax import lax
from jax.sharding import PartitionSpec as P

HEADS = 8


eps = 1e-05


def norm_rows(values):
    center = values - jnp.mean(values, axis=-1, keepdims=True)
    spread = jnp.mean(center * center, axis=-1, keepdims=True)
    return center * lax.rsqrt(spread + eps)


def pair_weights(seq_lengths, row_count):
    seq_ends = jnp.cumsum(seq_lengths)
    positions = jnp.arange(row_count, dtype=jnp.int32)
    segment = jnp.sum((positions[:, None] >= seq_ends[None, :]).astype(jnp.int32), axis=1)
    owned = segment[:, None] == jnp.arange(seq_lengths.shape[0], dtype=jnp.int32)[None, :]
    own_length = jnp.sum(jnp.where(owned, seq_lengths[None, :], 0), axis=1).astype(jnp.float32)
    allowed = (segment[:, None] == segment[None, :]) & (positions[None, :] <= positions[:, None])
    return jnp.where(allowed, 1.0 / own_length[:, None], 0.0)


def local_forward(embedded, w_uvqk, w_out, pair_weight):
    row_count, model_width = embedded.shape
    head_size = model_width // HEADS
    normed = norm_rows(embedded).astype(jnp.bfloat16)
    activated = jax.nn.silu(jnp.dot(normed, w_uvqk, preferred_element_type=jnp.float32)).astype(
        jnp.bfloat16
    )
    gate_part, value_part, query_part, key_part = jnp.split(activated, 4, axis=1)
    query_heads = query_part.reshape(row_count, HEADS, head_size)
    key_heads = key_part.reshape(row_count, HEADS, head_size)
    value_heads = value_part.reshape(row_count, HEADS, head_size)
    scores = jnp.einsum("qhe,khe->hqk", query_heads, key_heads, preferred_element_type=jnp.float32)
    attention = (jax.nn.silu(scores * head_size ** (-0.5)) * pair_weight[None]).astype(jnp.bfloat16)
    mixture = jnp.einsum("hqk,khe->qhe", attention, value_heads, preferred_element_type=jnp.float32)
    mixture = mixture.reshape(row_count, model_width)
    gated_rows = (norm_rows(mixture) * gate_part.astype(jnp.float32)).astype(jnp.bfloat16)
    return embedded + jnp.dot(gated_rows, w_out, preferred_element_type=jnp.float32)


def on_device(table, item_owner, item_row, lengths, cotangent, w_uvqk, w_out):
    wide_count = lax.axis_size("wide")
    rows_dev = table.shape[0]
    row_count, model_width = cotangent.shape
    capacity = 4 * row_count // wide_count
    owners = item_owner[:, 0]
    owner_onehot = (owners[:, None] == jnp.arange(wide_count, dtype=jnp.int32)[None, :]).astype(
        jnp.bfloat16
    )
    earlier = (jnp.arange(row_count)[:, None] > jnp.arange(row_count)[None, :]).astype(jnp.bfloat16)
    before = jnp.dot(earlier, owner_onehot, preferred_element_type=jnp.float32)
    within_rank = jnp.sum(before * owner_onehot.astype(jnp.float32), axis=1).astype(jnp.int32)
    slots = owners * capacity + within_rank
    requests = jnp.full((wide_count * capacity,), rows_dev, jnp.int32).at[slots].set(item_row)
    requests = requests.reshape(wide_count, capacity)
    asked = lax.all_to_all(requests, "wide", split_axis=0, concat_axis=0, tiled=True)
    picked = jnp.take(table, asked, axis=0, mode="fill", fill_value=0)
    replies = lax.all_to_all(picked, "wide", split_axis=0, concat_axis=0, tiled=True)
    embedded = replies.reshape(wide_count * capacity, model_width)[slots]
    pair_weight = pair_weights(lengths[0], row_count)

    def forward_rows(embed_rows, first_weight, second_weight):
        return local_forward(embed_rows, first_weight, second_weight, pair_weight)

    layer_out, pullback = jax.vjp(forward_rows, embedded.astype(jnp.float32), w_uvqk, w_out)
    grad_embed, grad_first, grad_second = pullback(cotangent.astype(jnp.float32))
    outgoing = (
        jnp.zeros((wide_count * capacity, model_width), jnp.float32).at[slots].set(grad_embed)
    )
    outgoing = outgoing.reshape(wide_count, capacity, model_width)
    arrived = lax.all_to_all(
        outgoing.astype(jnp.bfloat16), "wide", split_axis=0, concat_axis=0, tiled=True
    ).astype(outgoing.dtype)
    owner_sums = (
        jnp.zeros((rows_dev, model_width), jnp.float32)
        .at[asked.reshape(-1)]
        .add(arrived.reshape(-1, model_width), mode="drop")
    )
    grad_table = lax.psum(owner_sums.astype(jnp.bfloat16), "narrow").astype(jnp.float32)
    first_part, second_part = (
        lax.psum_scatter(
            grad_first.astype(jnp.float32).astype(jnp.bfloat16),
            "narrow",
            scatter_dimension=0,
            tiled=True,
        ).astype(jnp.float32),
        lax.psum_scatter(
            grad_second.astype(jnp.float32).astype(jnp.bfloat16),
            "narrow",
            scatter_dimension=0,
            tiled=True,
        ).astype(jnp.float32),
    )
    grad_uvqk, grad_out = (
        lax.psum_scatter(first_part, "wide", scatter_dimension=1, tiled=True),
        lax.psum_scatter(second_part, "wide", scatter_dimension=1, tiled=True),
    )
    return (grad_table, grad_uvqk, grad_out)


def solution(mesh):
    in_specs = (
        P("wide", None),
        P(("wide", "narrow"), None),
        P(("wide", "narrow")),
        P(("wide", "narrow"), None),
        P(("wide", "narrow"), None),
        P(),
        P(),
    )
    out_specs = (P("wide", None), P("narrow", "wide"), P("narrow", "wide"))
    return jax.shard_map(
        on_device, mesh=mesh, in_specs=in_specs, out_specs=out_specs, check_vma=False
    )
```

profile of v0, /device:TPU:1, one launch (start us, length us, event | category | flops | bytes accessed | tf_op | source)
XLA Modules:
  0.0 940.1 jit_solution(8000728038544306876)
XLA Ops:
  7.2 1.0 fusion.4
  8.2 0.7 fusion.40
  8.9 1.1 scatter_custom_fusion
  10.0 0.1 all_to_all.16
  10.1 32.2 %all_to_all.25 = s32[64,1,8]{2,1,0:T(1,128)S(1)} all-to-all(s32[64,1,8]{2,1,0:T(1,128)S(1)} %bitcast.88), channel_id=1, replica_groups=mesh['wide'=64,'narrow'=8] {'wide'}, dimensions={0} | all-to-all | bytes 4096 | tf_op jit(solution)/shard_map/all_to_all | solution.py:62
  42.3 0.1 reshape.272
  42.4 0.5 copy-done.8
  42.9 2.0 gather_fusion
  44.9 0.9 bitcast_select_fusion
  45.8 4.6 all-to-all-start.1
  50.5 0.2 reduce-window.8
  50.7 0.1 convert_reduce_fusion.1
  50.8 0.1 select_reduce_fusion
  50.9 0.1 fusion.35
  51.0 27.5 %all-to-all-done.1 = bf16[64,8,512]{2,1,0:T(8,128)(2,1)S(1)} async-done(((bf16[64,8,512]{2,1,0:T(8,128)(2,1)}), bf16[64,8,512]{2,1,0:T(8,128)(2,1)S(1)}, u32[]{:S(2)}, u32[]{:S(2)}) %all-to-all-start.1) | async-done | bytes 524320 | tf_op jit(solution)/shard_map/all_to_all | solution.py:64
  78.5 0.8 gather_fusion.1
  79.3 0.1 convert_reduce_fusion
  79.5 0.2 fusion.19
  79.7 1.5 multiply_convert_fusion
  81.2 0.1 copy.46
  81.4 0.1 copy.47
  81.5 0.8 copy.45
  82.3 1.1 multiply_convert_fusion.1
  83.4 0.3 fusion.51
  83.7 0.4 copy-done.5
  84.1 0.1 copy.48
  84.2 0.1 fusion.24
  84.3 1.5 multiply_reduce_fusion
  85.8 0.8 fusion.49
  86.7 0.1 broadcast_add_fusion
  86.8 0.1 copy.49
  86.9 0.2 fusion.54
  87.1 1.5 fusion.11
  88.6 0.3 fusion.53
  88.9 0.2 fusion.52
  89.1 0.1 copy.50
  89.2 0.1 copy.51
  89.3 0.1 copy.52
  89.5 3.4 convolution_convert_fusion
  93.0 2.2 fusion.21
  95.2 0.2 fusion.46
  95.4 0.5 copy-done.7
  95.9 0.5 negate_multiply_fusion
  96.4 1.9 scatter_custom_fusion.1
  98.3 0.9 convert_bitcast_fusion
  99.2 9.7 %all-to-all-start.2 = ((bf16[64,8,512]{2,1,0:T(8,128)(2,1)}), bf16[64,8,512]{2,1,0:T(8,128)(2,1)S(1)}, u32[]{:S(2)}, u32[]{:S(2)}) async-start(bf16[64,8,512]{2,1,0:T(8,128)(2,1)} %convert_bitcast_fusion), calls=%async_computation.2 | async-start | bytes 1048576 | tf_op jit(solution)/shard_map/all_to_all | solution.py:77
  108.9 0.0 reduce-scatter.9.cloned.1.call-start
  109.0 2.1 convolution_convert_fusion.1
  111.1 0.2 all-reduce.4.cloned.1.call-start
  111.3 0.5 broadcast.238
  111.9 0.7 reduce.6
  112.6 0.1 reshape.254
  112.7 24.1 %all-to-all-done.2 = bf16[64,8,512]{2,1,0:T(8,128)(2,1)S(1)} async-done(((bf16[64,8,512]{2,1,0:T(8,128)(2,1)}), bf16[64,8,512]{2,1,0:T(8,128)(2,1)S(1)}, u32[]{:S(2)}, u32[]{:S(2)}) %all-to-all-start.2) | async-done | bytes 524320 | tf_op jit(solution)/shard_map/all_to_all | solution.py:77
  136.8 3.8 scatter_custom_fusion.2
  140.6 0.7 convert_element_type.150
  141.4 0.0 reduce-scatter.11.cloned.1.call-start
  141.4 2.1 copy.55
  143.6 1.3 dynamic-slice
  145.5 24.9 %reduce-scatter.9.cloned.1.call-done = bf16[64,512]{1,0:T(8,128)(2,1)} async-done(((bf16[512,512]{1,0:T(8,128)(2,1)}), bf16[64,512]{1,0:T(8,128)(2,1)}) %reduce-scatter.9.cloned.1.call-update) | async-done | bytes 65552 | tf_op jit(solution)/shard_map/reduce_scatter | solution.py:93
  170.4 224.0 %all-reduce.5 = f32[64,512]{1,0:T(8,128)S(1)} all-reduce(bf16[64,512]{1,0:T(8,128)(2,1)} %reduce-scatter.9.cloned.1.call-done), channel_id=5, replica_groups=mesh['wide'=64,'narrow'=8] {'wide'}, use_global_device_ids=true, to_apply=%region_19.20.clone | all-reduce | flops 32768 | bytes 196608
  394.4 0.1 constant_dynamic-slice_fusion
  394.5 0.7 copy.54
  395.1 1.8 convert_element_type.151
  397.0 536.6 %reduce-scatter.11.cloned.1.call-done = f32[32,64]{1,0:T(8,128)} async-done(((f32[2048,64]{1,0:T(8,128)}), f32[32,64]{1,0:T(8,128)}) %reduce-scatter.11.cloned.1.call-update) | async-done | bytes 8208
  (57 shorter events, 0.3 us)
Async XLA Ops:
  7.2 72.5 %copy-start = (bf16[512,2048]{1,0:T(8,128)(2,1)S(1)}, bf16[512,2048]{1,0:T(8,128)(2,1)}, u32[]{:S(2)}) copy-start(bf16[512,2048]{1,0:T(8,128)(2,1)} %param.12) | copy-start | bytes 6291460
  7.2 35.7 %copy-start.1 = (bf16[256,512]{1,0:T(8,128)(2,1)S(1)}, bf16[256,512]{1,0:T(8,128)(2,1)}, u32[]{:S(2)}) copy-start(bf16[256,512]{1,0:T(8,128)(2,1)} %param.7) | copy-start | bytes 786436
  8.9 41.8 %copy-start.18 = (s32[128]{0:T(128)}, s32[128]{0:T(128)S(1)}, u32[]{:S(2)}) copy-start(s32[128]{0:T(128)S(1)} %fusion.40) | copy-start | bytes 1540
  42.3 0.6 copy-start.8
  44.9 5.6 copy-start.19
  45.8 32.7 %all-to-all-start.1 = ((bf16[64,8,512]{2,1,0:T(8,128)(2,1)}), bf16[64,8,512]{2,1,0:T(8,128)(2,1)S(1)}, u32[]{:S(2)}, u32[]{:S(2)}) async-start(bf16[64,8,512]{2,1,0:T(8,128)(2,1)} %bitcast_select_fusion), calls=%async_computation.1 | async-start | bytes 1048576 | tf_op jit(solution)/shard_map/all_to_all | solution.py:64
  50.5 91.0 %reduce-scatter.7.cloned.1.call-start = ((), (), s32[]{:S(2)}) async-start(), calls=%async_computation.7 | async-start | bytes 2359296 | tf_op jit(solution)/shard_map/reduce_scatter | solution.py:87
  51.0 31.3 %copy-start.14 = (f32[128,128]{1,0:T(8,128)}, f32[128,128]{1,0:T(8,128)S(1)}, u32[]{:S(2)}) copy-start(f32[128,128]{1,0:T(8,128)S(1)} %fusion.35) | copy-start | bytes 196612
  79.7 1.5 copy-start.16
  81.2 4.6 copy-start.4
  81.5 1.9 copy-start.10
  82.3 1.2 copy-start.12
  82.3 2.1 copy-start.2
  83.4 0.7 copy-start.5
  84.3 2.6 copy-start.6
  86.8 1.9 copy-start.11
  87.1 2.4 copy-start.13
  93.0 2.2 copy-start.17
  95.2 0.7 copy-start.7
  95.2 0.7 copy-start.15
  98.3 10.6 %copy-start.3 = (bf16[128,512]{1,0:T(8,128)(2,1)S(1)}, bf16[128,512]{1,0:T(8,128)(2,1)}, u32[]{:S(2)}) copy-start(bf16[128,512]{1,0:T(8,128)(2,1)} %param.11) | copy-start | bytes 393220
  99.2 12.7 %copy-start.9 = (s32[64,1,8]{2,1,0:T(1,128)S(1)}, s32[64,1,8]{2,1,0:T(1,128)}, u32[]{:S(2)}) copy-start(s32[64,1,8]{2,1,0:T(1,128)} %copy-done.8) | copy-start | bytes 6148
  99.2 37.6 %all-to-all-start.2 = ((bf16[64,8,512]{2,1,0:T(8,128)(2,1)}), bf16[64,8,512]{2,1,0:T(8,128)(2,1)S(1)}, u32[]{:S(2)}, u32[]{:S(2)}) async-start(bf16[64,8,512]{2,1,0:T(8,128)(2,1)} %convert_bitcast_fusion), calls=%async_computation.2 | async-start | bytes 1048576 | tf_op jit(solution)/shard_map/all_to_all | solution.py:77
  108.9 61.5 %reduce-scatter.9.cloned.1.call-start = ((), (), s32[]{:S(2)}) async-start(), calls=%async_computation.8 | async-start | bytes 589824 | tf_op jit(solution)/shard_map/reduce_scatter | solution.py:93
  111.1 284.0 %all-reduce.4.cloned.1.call-start = ((), (), s32[]{:S(2)}) async-start(), calls=%async_computation.6 | async-start | bytes 524288 | tf_op jit(solution)/shard_map/psum | solution.py:85
  141.4 792.2 %reduce-scatter.11.cloned.1.call-start = ((), (), s32[]{:S(2)}) async-start(), calls=%async_computation.9 | async-start | bytes 1064960
Sparse Core Ops, SparseCore 0:
  93.1 36.4 reduce-scatter.6
  132.4 37.9 reduce-scatter.8
  173.4 74.7 all-reduce.3
  253.0 680.5 reduce-scatter.10
where the time goes:
time: 951 us; the launch traced here: 940 us
  waiting for transfers between devices  613 us (64%)
  blocking collectives  256 us (27%)
  matrix products  15.4 us (2%)
  between operations  14.8 us (2%)
  starting transfers between devices  14.7 us (2%)
  other arithmetic  14 us (1%)
  local copies, waits for them, and re-layouts  11.9 us (1%)
    unnamed x5, waiting for transfers between devices  537 us
    unnamed x1, blocking collectives  224 us
    all_to_all x1, blocking collectives, on_device(): lax.all_to_all(requests, 'wide', split_axis=0, concat_axis=0, tiled=True)  32.2 us
    all_to_all x1, waiting for transfers between devices, on_device(): lax.all_to_all(picked, 'wide', split_axis=0, concat_axis=0, tiled=True)  27.5 us
    reduce_scatter x1, waiting for transfers between devices, on_device(): lax.psum_scatter(grad_second.astype(jnp.float32).astype(jnp.bfloat16), 'n...  24.9 us
    all_to_all x1, waiting for transfers between devices, on_device(): lax.all_to_all(outgoing.astype(jnp.bfloat16), 'wide', split_axis=0, conca...  24.1 us
  transfers between devices with their start and end apart: 6, of which 4 were waited for; matrix products, arithmetic and copies ran while one was open for 2% of the time, Pallas kernels for 0%

commit v1 on v0

v1 whole, which is shorter than its diff:
```python
import functools

import jax
import jax.numpy as jnp
from jax import lax
from jax.experimental import pallas as pl
from jax.experimental.pallas import tpu as pltpu
from jax.sharding import PartitionSpec as P

HEADS = 8
EPS = 1e-05
MESH = pl.DeviceIdType.MESH
F32, BF16, I32 = jnp.float32, jnp.bfloat16, jnp.int32
VMEM_LIMIT = 48 * 1024 * 1024


def div(value, by):
    return lax.div(value, jnp.int32(by))


def rem(value, by):
    return lax.rem(value, jnp.int32(by))


def coordinates():
    wide, narrow = lax.axis_index("wide"), lax.axis_index("narrow")
    return div(wide, 16), rem(wide, 16), div(narrow, 2), rem(narrow, 2)


def shard_z(y, c, b):
    return 2 * (rem(y + 2 * b, 4) + 4 * c) + 1 - b


def holder_of(z):
    b = 1 - rem(z, 2)
    half = div(z, 2)
    y = rem(rem(half, 4) + 4 - 2 * b, 4)
    return 2 * y + div(half, 4), b


def member(rank, a):
    narrow, b = holder_of(rem(rank, 16))
    return div(rank, 16) * 16 + 2 * a + b, narrow


def signal(sem, device):
    pl.semaphore_signal(sem, inc=1, device_id=device, device_id_type=MESH)


def send(src, dst, send_sem, recv_sem, device):
    pltpu.make_async_remote_copy(
        src_ref=src, dst_ref=dst, send_sem=send_sem, recv_sem=recv_sem, device_id=device, device_id_type=MESH
    ).start()


def waiter(ref, send_sem, recv_sem, device):
    return pltpu.make_async_remote_copy(
        src_ref=ref, dst_ref=ref, send_sem=send_sem, recv_sem=recv_sem, device_id=device, device_id_type=MESH
    )


def iota(shape, dim):
    return lax.broadcasted_iota(I32, shape, dim)


def onehot(hits):
    return jnp.where(hits, 1.0, 0.0).astype(BF16)


def dot(left, right, contract=((1,), (0,))):
    return lax.dot_general(left, right, (contract, ((), ())), preferred_element_type=F32)


def ranks(owner_c, owner_r):
    sub, lane = iota((128, 128), 0), iota((128, 128), 1)
    same = owner_c == owner_r
    across = jnp.sum(jnp.where(same & (sub < lane), 1.0, 0.0), axis=0, keepdims=True)
    down = jnp.sum(jnp.where(same & (lane < sub), 1.0, 0.0), axis=1, keepdims=True)
    return down.astype(I32), across.astype(I32)


def halves_to_blocks(first, second):
    return jnp.concatenate([first.reshape(64, 8, 256), second.reshape(64, 8, 256)], axis=1).astype(BF16)


def fetch_kernel(
    owner_c, owner_r, row_c, table, replies, asked,
    shard, ask_out, reply_out, shard_send, shard_recv, ask_send, ask_recv, reply_send, reply_recv,
):
    x, z, y, c = coordinates()
    a, b = div(z, 2), rem(z, 2)
    narrow = 2 * y + c
    my_z = shard_z(y, c, b)
    me = x * 16 + my_z
    to_narrow, to_b = holder_of(z)
    is_source = to_narrow == narrow
    barrier = pltpu.get_barrier_semaphore()

    def greet(step, carry):
        signal(barrier, member(rem(me + step, 64), a))
        return carry

    lax.fori_loop(1, 64, greet, 0)
    signal(barrier, (x * 16 + my_z, narrow))

    _, rank_r = ranks(owner_c[...], owner_r[...])
    slots = onehot(iota((512, 128), 0) == owner_r[...] * 8 + rank_r)
    named = jnp.broadcast_to((row_c[...] + 1).astype(F32), (128, 128)).astype(BF16)
    ask_out[...] = dot(slots, named).reshape(64, 8, 128)

    pl.semaphore_wait(barrier, 63 + 8 * is_source.astype(I32))

    @pl.when(is_source)
    def _():
        def give(step, carry):
            for half in range(2):
                send(
                    table.at[:, pl.ds(256 * half, 256)], shard.at[half],
                    shard_send.at[half], shard_recv.at[half], (x * 16 + 2 * step + to_b, narrow),
                )
            return carry

        lax.fori_loop(0, 8, give, 0)

    def ask(step, carry):
        rank = rem(me + step, 64)
        send(ask_out.at[rank], asked.at[me], ask_send, ask_recv, member(rank, a))
        return carry

    lax.fori_loop(1, 64, ask, 0)
    asked[pl.ds(me, 1)] = ask_out[pl.ds(me, 1)]
    here = (lax.axis_index("wide"), narrow)
    most = asked.at[pl.ds(0, 63)]
    waiter(most, ask_send, ask_recv, here).wait_recv()
    wanted = asked[...].reshape(512, 128).astype(I32)
    wanted = jnp.concatenate([wanted, wanted], axis=1)
    chosen = onehot(wanted == iota((512, 256), 1) + 1)
    for half in range(2):
        waiter(shard.at[half], shard_send.at[half], shard_recv.at[half], here).wait_recv()
    reply_out[...] = halves_to_blocks(dot(chosen, shard[0]), dot(chosen, shard[1]))

    def answer(step, carry):
        rank = rem(me + step, 64)
        send(reply_out.at[rank], replies.at[me], reply_send, reply_recv, member(rank, a))
        return carry

    lax.fori_loop(1, 64, answer, 0)
    replies[pl.ds(me, 1)] = reply_out[pl.ds(me, 1)]
    waiter(most, ask_send, ask_recv, here).wait_send()

    @pl.when(is_source)
    def _():
        def given(step, carry):
            for half in range(2):
                waiter(shard.at[half], shard_send.at[half], shard_recv.at[half], here).wait_send()
            return carry

        lax.fori_loop(0, 8, given, 0)

    waiter(replies.at[pl.ds(0, 63)], reply_send, reply_recv, here).wait()


def mean_rows(values):
    return jnp.mean(values, axis=-1, keepdims=True)


def norm_back(grad, normed, scale):
    return scale * (grad - mean_rows(grad) - normed * mean_rows(grad * normed))


def layer_kernel(lengths, owner_c, owner_r, replies, cotangent, w_uvqk, w_out, outgoing, grad_u, grad_o, pre, act, grad_act):
    rank_c, rank_r = ranks(owner_c[...], owner_r[...])
    slot_c = owner_c[...] * 16 + rank_c
    spots = iota((128, 1024), 1)
    arrived = replies[...]
    embedded = jnp.concatenate(
        [dot(onehot(spots == slot_c), arrived), dot(onehot(spots == slot_c + 8), arrived)], axis=1
    )
    center = embedded - mean_rows(embedded)
    embed_scale = lax.rsqrt(mean_rows(center * center) + EPS)
    embed_norm = center * embed_scale
    normed = embed_norm.astype(BF16)

    for part in range(4):
        cols = pl.ds(512 * part, 512)
        value = dot(normed, w_uvqk[:, cols])
        pre[:, cols] = value
        act[:, cols] = (value * jax.nn.sigmoid(value)).astype(BF16)

    sub, lane = iota((128, 128), 0), iota((128, 128), 1)
    seg_t, seg_s, total = jnp.zeros((128, 128), I32), jnp.zeros((128, 128), I32), jnp.int32(0)
    for i in range(6):
        total = total + lengths[0, i]
        seg_t = seg_t + jnp.where(sub >= total, 1, 0)
        seg_s = seg_s + jnp.where(lane >= total, 1, 0)
    own_length = jnp.ones((128, 128), F32)
    for i in range(6):
        own_length = jnp.where(seg_t == i, lengths[0, i].astype(F32), own_length)
    weight = jnp.where((seg_t == seg_s) & (lane <= sub), 1.0 / own_length, 0.0)

    first_half = lane < 64
    keep = (first_half, jnp.logical_not(first_half))
    zero = jnp.zeros((128, 128), BF16)
    mixed = []
    for pair in range(4):
        q = act[:, 1024 + 128 * pair : 1152 + 128 * pair]
        k = act[:, 1536 + 128 * pair : 1664 + 128 * pair]
        v = act[:, 512 + 128 * pair : 640 + 128 * pair]
        both = jnp.zeros((128, 128), F32)
        for head in range(2):
            score = dot(jnp.where(keep[head], q, zero), k, ((1,), (1,))) * 0.125
            attention = (score * jax.nn.sigmoid(score) * weight).astype(BF16)
            both = both + dot(attention, jnp.where(keep[head], v, zero))
        mixed.append(both)
    mixture = jnp.concatenate(mixed, axis=1)
    center = mixture - mean_rows(mixture)
    mix_scale = lax.rsqrt(mean_rows(center * center) + EPS)
    mix_norm = center * mix_scale
    gate = act[:, 0:512].astype(F32)
    gated = (mix_norm * gate).astype(BF16)

    cot = cotangent[...]
    grad_o[...] = dot(cot, gated, ((0,), (0,))).astype(BF16)
    grad_gated = dot(cot, w_out[...], ((1,), (1,)))
    grad_act[:, 0:512] = grad_gated * mix_norm
    grad_mix = norm_back(grad_gated * gate, mix_norm, mix_scale).astype(BF16)
    for pair in range(4):
        q = act[:, 1024 + 128 * pair : 1152 + 128 * pair]
        k = act[:, 1536 + 128 * pair : 1664 + 128 * pair]
        v = act[:, 512 + 128 * pair : 640 + 128 * pair]
        g = grad_mix[:, 128 * pair : 128 * pair + 128]
        grad_q, grad_k, grad_v = [jnp.zeros((128, 128), F32)] * 3
        for head in range(2):
            q_one, k_one, v_one, g_one = [jnp.where(keep[head], part, zero) for part in (q, k, v, g)]
            score = dot(q_one, k, ((1,), (1,))) * 0.125
            gain = jax.nn.sigmoid(score)
            attention = (score * gain * weight).astype(BF16)
            grad_att = dot(g_one, v, ((1,), (1,)))
            grad_score = (grad_att * weight * (gain * (1.0 + score * (1.0 - gain))) * 0.125).astype(BF16)
            grad_v = grad_v + dot(attention, g_one, ((0,), (0,)))
            grad_q = grad_q + dot(grad_score, k_one)
            grad_k = grad_k + dot(grad_score, q_one, ((0,), (0,)))
        grad_act[:, 512 + 128 * pair : 640 + 128 * pair] = grad_v
        grad_act[:, 1024 + 128 * pair : 1152 + 128 * pair] = grad_q
        grad_act[:, 1536 + 128 * pair : 1664 + 128 * pair] = grad_k

    grad_normed = jnp.zeros((128, 512), F32)
    for part in range(4):
        cols = pl.ds(512 * part, 512)
        value = pre[:, cols]
        gain = jax.nn.sigmoid(value)
        grad_pre = (grad_act[:, cols] * (gain * (1.0 + value * (1.0 - gain)))).astype(BF16)
        grad_normed = grad_normed + dot(grad_pre, w_uvqk[:, cols], ((1,), (1,)))
        grad_u[cols, :] = dot(grad_pre, normed, ((0,), (0,))).astype(BF16)
    grad_embed = cot.astype(F32) + norm_back(grad_normed, embed_norm, embed_scale)
    grad_embed = grad_embed.astype(BF16)
    slots = onehot(iota((512, 128), 0) == owner_r[...] * 8 + rank_r)
    outgoing[...] = halves_to_blocks(dot(slots, grad_embed[:, 0:256]), dot(slots, grad_embed[:, 256:512]))


def reduce_kernel(
    outgoing, asked, grad_u, grad_o, out_table, out_u, out_o,
    rows_in, pair_in, plane_out, plane_in, line_out, line_in, piece_out, piece_in, share, turned,
    rows_send, rows_recv, pair_send, pair_recv, plane_send, plane_recv, line_send, line_recv,
    piece_send, piece_recv, share_send, share_recv,
):
    x, z, y, c = coordinates()
    wide = x * 16 + z
    a, b = div(z, 2), rem(z, 2)
    narrow = 2 * y + c
    my_z = shard_z(y, c, b)
    me = x * 16 + my_z
    from_narrow, from_b = holder_of(z)
    upper = div(z, 8)
    here = (wide, narrow)
    in_half = (upper == c).astype(I32)
    barrier = pltpu.get_barrier_semaphore()

    def greet(step, carry):
        signal(barrier, member(rem(me + step, 64), a))
        return carry

    lax.fori_loop(1, 64, greet, 0)

    def greet_line(step, carry):
        signal(barrier, (x * 16 + 2 * step + from_b, from_narrow))
        return carry

    lax.fori_loop(0, 8, greet_line, 0)

    def greet_column(step, carry):
        @pl.when(jnp.logical_or(step != z, upper != c))
        def _():
            signal(barrier, (x * 16 + step, 2 * y + upper))

        return carry

    lax.fori_loop(0, 16, greet_column, 0)
    pl.semaphore_wait(barrier, 63 + 8 + 16 - in_half)

    partner = (wide, 2 * y + 1 - c)
    for part in range(4):
        send(
            grad_u.at[pl.ds(512 * part + 256 * (1 - c), 256)], pair_in.at[part, pl.ds(0, 256)],
            pair_send, pair_recv, partner,
        )
        send(
            grad_o.at[pl.ds(128 * part + 64 * (1 - c), 64)], pair_in.at[part, pl.ds(256, 64)],
            pair_send, pair_recv, partner,
        )

    def give_rows(step, carry):
        rank = rem(me + step, 64)
        send(outgoing.at[rank], rows_in.at[me], rows_send, rows_recv, member(rank, a))
        return carry

    lax.fori_loop(1, 64, give_rows, 0)
    rows_in[pl.ds(me, 1)] = outgoing[pl.ds(me, 1)]

    waiter(pair_in, pair_send, pair_recv, here).wait()
    for part in range(4):
        mine = grad_u[pl.ds(512 * part + 256 * c, 256), :].astype(F32)
        plane_out[part, 0:256] = (mine + pair_in[part, 0:256].astype(F32)).astype(BF16)
        mine = grad_o[pl.ds(128 * part + 64 * c, 64), :].astype(F32)
        plane_out[part, 256:320] = (mine + pair_in[part, 256:320].astype(F32)).astype(BF16)

    spot = 4 * x + y

    def give_plane(step, carry):
        to = rem(spot + step, 16)
        to_x, to_y = div(to, 4), rem(to, 4)
        send(
            plane_out.at[to_x, :, pl.ds(pl.multiple_of(128 * to_y, 128), 128)], plane_in.at[spot],
            plane_send, plane_recv, (to_x * 16 + z, 2 * to_y + c),
        )
        return carry

    lax.fori_loop(1, 16, give_plane, 0)
    plane_in[pl.ds(spot, 1)] = plane_out[pl.ds(x, 1), :, pl.ds(pl.multiple_of(128 * y, 128), 128)]

    waiter(rows_in.at[pl.ds(0, 63)], rows_send, rows_recv, here).wait()
    wanted = asked[...].reshape(512, 128).astype(I32)
    wanted = jnp.concatenate([wanted, wanted], axis=1)
    chosen = onehot(wanted == iota((512, 256), 1) + 1)
    arrived = rows_in[...].astype(F32)
    for half in range(2):
        rows = arrived[:, 8 * half : 8 * half + 8].reshape(512, 256).astype(BF16)
        sums = dot(chosen, rows, ((0,), (0,))).astype(BF16)
        for piece in range(8):
            piece_out[piece, 32 * half : 32 * half + 32] = sums[32 * piece : 32 * piece + 32]

    def give_piece(step, carry):
        to = rem(narrow + step, 8)
        send(piece_out.at[to], piece_in.at[a], piece_send, piece_recv, (x * 16 + my_z, to))
        return carry

    lax.fori_loop(0, 8, give_piece, 0)

    waiter(plane_in.at[pl.ds(0, 15)], plane_send, plane_recv, here).wait()
    total = plane_in[0].astype(F32)
    for step in range(1, 16):
        total = total + plane_in[step].astype(F32)
    for step in range(8):
        line_out[step] = jnp.concatenate(
            [total[32 * step : 32 * step + 32], total[256 + 8 * step : 264 + 8 * step], jnp.zeros((8, 128), F32)], axis=0
        ).astype(BF16)

    def give_line(step, carry):
        to_z = 8 * c + step
        for core in range(2):
            own = jnp.logical_and(to_z == z, c == core)

            @pl.when(jnp.logical_not(own))
            def _():
                send(line_out.at[step], line_in.at[z], line_send, line_recv, (x * 16 + to_z, 2 * y + core))

            @pl.when(own)
            def _():
                line_in[pl.ds(z, 1)] = line_out[pl.ds(step, 1)]

        return carry

    lax.fori_loop(0, 8, give_line, 0)

    waiter(piece_in, piece_send, piece_recv, here).wait()
    total = piece_in[0].astype(F32)
    for step in range(1, 8):
        total = total + piece_in[step].astype(F32)
    share[pl.ds(narrow, 1)] = total.astype(BF16).reshape(1, 64, 256)

    def give_share(step, carry):
        send(share.at[narrow], share.at[narrow], share_send, share_recv, (wide, rem(narrow + step, 8)))
        return carry

    lax.fori_loop(1, 8, give_share, 0)

    @pl.when(in_half == 1)
    def _():
        waiter(line_in.at[pl.ds(0, 15)], line_send, line_recv, here).wait()

    @pl.when(in_half == 0)
    def _():
        waiter(line_in, line_send, line_recv, here).wait()

    total = line_in[0].astype(F32)
    for step in range(1, 16):
        total = total + line_in[step].astype(F32)
    turned[...] = jnp.concatenate([total, jnp.zeros((80, 128), F32)], axis=0).T
    mine = turned[pl.ds(pl.multiple_of(64 * c, 64), 64), :]
    out_u[...] = mine[:, 0:32]
    out_o[...] = mine[:, 32:40]

    waiter(share.at[pl.ds(0, 7)], share_send, share_recv, here).wait()
    for piece in range(8):
        out_table[32 * piece : 32 * piece + 32, 0:256] = share[piece, 0:32].astype(F32)
        out_table[32 * piece : 32 * piece + 32, 256:512] = share[piece, 32:64].astype(F32)


def on_device(table, item_owner, item_row, lengths, cotangent, w_uvqk, w_out):
    owner_c, owner_r, row_c = item_owner, item_owner.reshape(1, 128), item_row.reshape(128, 1)
    vmem = pl.BlockSpec(memory_space=pltpu.VMEM)
    smem = pl.BlockSpec(memory_space=pltpu.SMEM)
    dma = pltpu.SemaphoreType.DMA
    shape = jax.ShapeDtypeStruct

    replies, asked = pl.pallas_call(
        fetch_kernel,
        out_shape=(shape((64, 16, 256), BF16), shape((64, 8, 128), F32)),
        in_specs=[vmem] * 4,
        out_specs=(vmem, vmem),
        scratch_shapes=[
            pltpu.VMEM((2, 256, 256), BF16),
            pltpu.VMEM((64, 8, 128), F32),
            pltpu.VMEM((64, 16, 256), BF16),
            dma((2,)), dma((2,)), dma, dma, dma, dma,
        ],
        compiler_params=pltpu.CompilerParams(collective_id=0, has_side_effects=True, vmem_limit_bytes=VMEM_LIMIT),
        name="fetch_rows",
    )(owner_c, owner_r, row_c, table)

    outgoing, grad_u, grad_o = pl.pallas_call(
        layer_kernel,
        out_shape=(shape((64, 16, 256), BF16), shape((2048, 512), BF16), shape((512, 512), BF16)),
        in_specs=[smem] + [vmem] * 6,
        out_specs=(vmem,) * 3,
        scratch_shapes=[pltpu.VMEM((128, 2048), F32), pltpu.VMEM((128, 2048), BF16), pltpu.VMEM((128, 2048), F32)],
        compiler_params=pltpu.CompilerParams(vmem_limit_bytes=VMEM_LIMIT),
        name="layer",
    )(lengths, owner_c, owner_r, replies.reshape(1024, 256), cotangent, w_uvqk, w_out)

    return pl.pallas_call(
        reduce_kernel,
        out_shape=(shape((256, 512), F32), shape((64, 32), F32), shape((64, 8), F32)),
        in_specs=[vmem] * 4,
        out_specs=(vmem,) * 3,
        scratch_shapes=[
            pltpu.VMEM((64, 16, 256), BF16),
            pltpu.VMEM((4, 320, 512), BF16),
            pltpu.VMEM((4, 320, 512), BF16),
            pltpu.VMEM((16, 320, 128), BF16),
            pltpu.VMEM((8, 48, 128), BF16),
            pltpu.VMEM((16, 48, 128), BF16),
            pltpu.VMEM((8, 64, 256), BF16),
            pltpu.VMEM((8, 64, 256), BF16),
            pltpu.VMEM((8, 64, 256), BF16),
            pltpu.VMEM((128, 128), F32),
        ] + [dma] * 12,
        compiler_params=pltpu.CompilerParams(collective_id=1, has_side_effects=True, vmem_limit_bytes=VMEM_LIMIT),
        name="reduce_grads",
    )(outgoing, asked, grad_u, grad_o)


def solution(mesh):
    in_specs = (
        P("wide", None),
        P(("wide", "narrow"), None),
        P(("wide", "narrow")),
        P(("wide", "narrow"), None),
        P(("wide", "narrow"), None),
        P(),
        P(),
    )
    out_specs = (P("wide", None), P("narrow", "wide"), P("narrow", "wide"))
    return jax.shard_map(on_device, mesh=mesh, in_specs=in_specs, out_specs=out_specs, check_vma=False)
```

time: 951 us -> 117 us (0.12); the launches traced: 940 us -> 116 us
  waiting for transfers between devices: 613 us -> 0 us
  blocking collectives: 256 us -> 0 us
  Pallas kernels: 0 us -> 108 us
  matrix products: 15.4 us -> 0 us
  starting transfers between devices: 14.7 us -> 0 us
  between operations: 14.8 us -> 0.67 us
  other arithmetic: 14 us -> 0 us
    unnamed x5 -> x0, waiting for transfers between devices: 537 us -> none
    unnamed x1 -> x0, blocking collectives: 224 us -> none
    pallas_call x0 -> x3, Pallas kernels: none -> 108 us  [the longest x1 50.9 us: on_device(): pl.pallas_call(reduce_kernel, out_shape=(shape((256, 512), F32), shape((6...]
    all_to_all x2 -> x0, waiting for transfers between devices: 51.6 us -> none  [the longest x1 27.5 us: on_device(): lax.all_to_all(picked, 'wide', split_axis=0, concat_axis=0, tiled=True)]
    all_to_all x1 -> x0, blocking collectives: 32.2 us -> none  [on_device(): lax.all_to_all(requests, 'wide', split_axis=0, concat_axis=0, tiled=True)]
    reduce_scatter x2 -> x0, waiting for transfers between devices: 24.9 us -> none  [the longest x1 24.9 us: on_device(): lax.psum_scatter(grad_second.astype(jnp.float32).astype(jnp.bfloat16), 'n...]
    dot_general x12 -> x0, matrix products: 15.4 us -> none  [the longest x3 7.16 us: local_forward(): jnp.dot(normed, w_uvqk, preferred_element_type=jnp.float32)]
    all_to_all x2 -> x0, starting transfers between devices: 14.3 us -> none  [the longest x1 9.71 us: on_device(): lax.all_to_all(outgoing.astype(jnp.bfloat16), 'wide', split_axis=0, conca...]
  transfers between devices with their start and end apart: 6 -> 0, of which waited for: 4 -> 0; matrix products, arithmetic and copies ran while one was open for 2% -> 0% of each run, Pallas kernels for 0% -> 0%
where the time goes in v1:
time: 117 us; the launch traced here: 116 us
  Pallas kernels  108 us (92%)
  local copies, waits for them, and re-layouts  7.85 us (7%)
    pallas_call x1, Pallas kernels, on_device(): pl.pallas_call(reduce_kernel, out_shape=(shape((256, 512), F32), shape((6...  50.9 us
    pallas_call x1, Pallas kernels, on_device(): pl.pallas_call(fetch_kernel, out_shape=(shape((64, 16, 256), BF16), shape...  50.2 us
    pallas_call x1, Pallas kernels, on_device(): pl.pallas_call(layer_kernel, out_shape=(shape((64, 16, 256), BF16), shape...  6.77 us
    unnamed x12, local copies, waits for them, and re-layouts  5.75 us

profile of v1, /device:TPU:1, one launch (start us, length us, event | category | flops | bytes accessed | tf_op | source)
XLA Modules:
  0.0 116.4 jit_solution(12309702020247406836)
XLA Ops:
  0.6 0.8 copy.12.owner_c
  1.4 0.8 copy.11.row_c
  2.2 0.0 copy-start.1
  2.2 0.9 copy-done.1
  3.1 0.0 copy-start.3
  3.1 0.7 copy-done.3
  3.8 50.2 %fetch_rows.1 = (bf16[64,16,256]{2,1,0:T(8,128)(2,1)S(1)}, f32[64,8,128]{2,1,0:T(8,128)S(1)}) custom-call(s32[128,1]{1,0:T(8,128)S(1)} %copy.12.owner_c, s32[1,128]{1,0:T(1,128)S(1)} %bitcast.4, s32[128,1]{1,0:T(8,128)S(1)} %copy.11.row_c, bf16[256,512]{1,0:T(8,128)(2,1)S(1)} %copy-done.1), custom_call_target="tpu_custom_call" | custom-call | tf_op jit(solution)/shard_map/fetch_rows/pallas_call | solution.py:426
  53.9 0.0 copy-start
  54.0 1.0 copy-done
  55.0 0.0 copy-start.2
  55.0 0.9 copy-done.2
  55.9 0.0 copy-start.4
  55.9 0.7 copy-done.4
  56.5 6.8 %layer.1 = (bf16[64,16,256]{2,1,0:T(8,128)(2,1)S(1)}, bf16[2048,512]{1,0:T(8,128)(2,1)S(1)}, bf16[512,512]{1,0:T(8,128)(2,1)S(1)}) custom-call(s32[1,6]{1,0:T(1,128)S(1)} %copy-done.4, s32[128,1]{1,0:T(8,128)S(1)} %copy.12.owner_c, s32[1,128]{1,0:T(1,128)S(1)} %bitcast.5, bf16[1024,256]{1,0:T(8,128)(2,1)S(1)} %bitcast.3, bf16[128,512]{1,0:T(8,128)(2,1)S(1)} %copy-done.2, ...), custom_call_target="tpu_custom_call" | custom-call | tf_op jit(solution)/shard_map/layer/pallas_call | solution.py:441
  63.3 50.9 %reduce_grads.1 = (f32[256,512]{1,0:T(8,128)S(1)}, f32[64,32]{1,0:T(8,128)S(1)}, f32[64,8]{1,0:T(8,128)S(1)}) custom-call(bf16[64,16,256]{2,1,0:T(8,128)(2,1)S(1)} %get-tuple-element.9.outgoing, f32[64,8,128]{2,1,0:T(8,128)S(1)} %get-tuple-element.10.asked, bf16[2048,512]{1,0:T(8,128)(2,1)S(1)} %get-tuple-element.11.grad_u, ...), custom_call_target="tpu_custom_call" | custom-call | tf_op jit(solution)/shard_map/reduce_grads/pallas_call | solution.py:451
  114.2 0.7 copy.14
  114.9 0.7 copy.13
  115.6 0.8 copy.16
Async XLA Ops:
  2.2 0.9 copy-start.1
  3.1 0.7 copy-start.3
  53.9 1.0 copy-start
  55.0 0.9 copy-start.2
  55.9 0.7 copy-start.4

commit v2 on v0

v2 whole, which is shorter than its diff:
```python
import jax
import jax.numpy as jnp
from jax import lax
from jax.experimental import pallas as pl
from jax.experimental.pallas import tpu as pltpu
from jax.sharding import PartitionSpec as P

HEADS = 8
EPS = 1e-05
MESH = pl.DeviceIdType.MESH
F32, BF16, I32 = jnp.float32, jnp.bfloat16, jnp.int32
VMEM_LIMIT = 63 * 1024 * 1024


def div(value, by):
    return lax.div(value, jnp.int32(by))


def rem(value, by):
    return lax.rem(value, jnp.int32(by))


def coordinates():
    wide, narrow = lax.axis_index("wide"), lax.axis_index("narrow")
    return div(wide, 16), rem(wide, 16), div(narrow, 2), rem(narrow, 2)


def shard_z(y, c, b):
    return 2 * (rem(y + 2 * b, 4) + 4 * c) + 1 - b


def holder_of(z):
    b = 1 - rem(z, 2)
    half = div(z, 2)
    y = rem(rem(half, 4) + 4 - 2 * b, 4)
    return 2 * y + div(half, 4), b


def member(rank, a):
    narrow, b = holder_of(rem(rank, 16))
    return div(rank, 16) * 16 + 2 * a + b, narrow


def signal(sem, device):
    pl.semaphore_signal(sem, inc=1, device_id=device, device_id_type=MESH)


def send(src, dst, send_sem, recv_sem, device):
    pltpu.make_async_remote_copy(
        src_ref=src, dst_ref=dst, send_sem=send_sem, recv_sem=recv_sem, device_id=device, device_id_type=MESH
    ).start()


def waiter(ref, send_sem, recv_sem, device):
    return pltpu.make_async_remote_copy(
        src_ref=ref, dst_ref=ref, send_sem=send_sem, recv_sem=recv_sem, device_id=device, device_id_type=MESH
    )


def iota(shape, dim):
    return lax.broadcasted_iota(I32, shape, dim)


def onehot(hits):
    return jnp.where(hits, 1.0, 0.0).astype(BF16)


def dot(left, right, contract=((1,), (0,))):
    return lax.dot_general(left, right, (contract, ((), ())), preferred_element_type=F32)


def ranks(owner_t, owner_s):
    sub, lane = iota((128, 128), 0), iota((128, 128), 1)
    same = owner_t == owner_s
    across = jnp.sum(jnp.where(same & (sub < lane), 1.0, 0.0), axis=0, keepdims=True)
    down = jnp.sum(jnp.where(same & (lane < sub), 1.0, 0.0), axis=1, keepdims=True)
    return down, across


def to_blocks(first, second):
    return jnp.concatenate([first.reshape(64, 8, 128), second.reshape(64, 8, 128)], axis=1).astype(BF16)


def from_blocks(blocks):
    values = blocks.astype(F32)
    return jnp.concatenate([values[:, 0:8].reshape(512, 128), values[:, 8:16].reshape(512, 128)], axis=1).astype(BF16)


def mean_rows(values):
    return jnp.mean(values, axis=-1, keepdims=True)


def norm_back(grad, normed, scale):
    return scale * (grad - mean_rows(grad) - normed * mean_rows(grad * normed))


def weights_of_pairs(lengths):
    sub, lane = iota((128, 128), 0), iota((128, 128), 1)
    seg_t, seg_s = jnp.zeros((128, 128), I32), jnp.zeros((128, 128), I32)
    total = jnp.zeros((1, 1), I32)
    for i in range(6):
        total = total + lengths[0:1, i : i + 1]
        seg_t = seg_t + jnp.where(sub >= total, 1, 0)
        seg_s = seg_s + jnp.where(lane >= total, 1, 0)
    own_length = jnp.ones((128, 128), F32)
    for i in range(6):
        own_length = jnp.where(seg_t == i, lengths[0:1, i : i + 1].astype(F32), own_length)
    return jnp.where((seg_t == seg_s) & (lane <= sub), 1.0 / own_length, 0.0)


def layer_kernel(
    owner_hbm, row_hbm, lengths_hbm, table, cotangent_hbm, w_uvqk_hbm, w_out_hbm, out_table, out_u, out_o,
    owner, row, lengths, cotangent, w_uvqk, w_out, shard, ask_out, asked, chosen, reply_out, replies,
    pre, act, grad_act, grads, rows_out, rows_in, pair_in, plane_out, x_in, y_in, x_mid, y_mid, xy_in, yx_in,
    line_out, line_in, piece_out, piece_in, share, turned,
    load_sem, shard_send, shard_recv, relay_send, ask_send, ask_recv, reply_send, reply_recv,
    rows_send, rows_recv, pair_send, pair_recv, plane_send, plane_recv, line_send, line_recv,
    piece_send, piece_recv, share_send, share_recv,
):
    x, z, y, c = coordinates()
    wide = x * 16 + z
    a, b = div(z, 2), rem(z, 2)
    narrow = 2 * y + c
    here = (wide, narrow)
    my_z = shard_z(y, c, b)
    me = x * 16 + my_z
    to_narrow, to_b = holder_of(z)
    is_source = to_narrow == narrow
    away = rem(z - my_z + 16, 16)
    is_relay = jnp.logical_or(away == 3, away == 13)
    outward = jnp.where(away == 3, 1, -1)
    upper = div(z, 8)
    in_half = (upper == c).astype(I32)
    barrier = pltpu.get_barrier_semaphore()

    def on_line(at_z):
        return x * 16 + rem(at_z + 32, 16), narrow

    loads = []
    for i, (src, dst) in enumerate(
        [(owner_hbm, owner), (row_hbm, row), (lengths_hbm, lengths), (w_uvqk_hbm, w_uvqk), (cotangent_hbm, cotangent), (w_out_hbm, w_out)]
    ):
        loads.append(pltpu.make_async_copy(src, dst, load_sem.at[i]))
        loads[-1].start()

    parent = jnp.where(
        jnp.logical_or(away == 5, away == 7), my_z + 3, jnp.where(jnp.logical_or(away == 9, away == 11), my_z - 3, my_z)
    )
    signal(barrier, on_line(parent))

    def greet_line(step, carry):
        signal(barrier, (x * 16 + 2 * step + to_b, to_narrow))
        return carry

    lax.fori_loop(0, 8, greet_line, 0)

    def greet_column(step, carry):
        @pl.when(jnp.logical_or(step != z, upper != c))
        def _():
            signal(barrier, (x * 16 + step, 2 * y + upper))

        return carry

    lax.fori_loop(0, 16, greet_column, 0)

    def greet(step, carry):
        signal(barrier, member(rem(me + step, 64), a))
        return carry

    lax.fori_loop(1, 64, greet, 0)

    loads[0].wait()
    loads[1].wait()
    owner_s = jnp.broadcast_to(owner[...].astype(F32), (128, 128))
    owner_t = owner_s.T
    rank_t, rank_s = ranks(owner_t, owner_s)
    slot_s = (owner_s * 8.0 + rank_s)[0:1].astype(I32)
    slot_t = (owner_t * 16.0 + rank_t)[:, 0:1].astype(I32)
    slots = onehot(iota((512, 128), 0) == slot_s)
    named = (jnp.broadcast_to(row[...].astype(F32), (128, 128)).T + 1.0).astype(BF16)
    ask_out[...] = dot(slots, named).reshape(64, 8, 128)

    pl.semaphore_wait(barrier, 63 + 8 + 16 - in_half + 4 * is_source.astype(I32) + 2 * is_relay.astype(I32))

    for half in range(2):

        @pl.when(is_source)
        def _(half=half):
            for step in (3, -3, 1, -1):
                send(
                    table.at[:, pl.ds(256 * half, 256)], shard.at[half],
                    shard_send.at[half], shard_recv.at[half], on_line(z + step),
                )

    def ask(step, carry):
        rank = rem(me + step, 64)
        send(ask_out.at[rank], asked.at[me], ask_send, ask_recv, member(rank, a))
        return carry

    lax.fori_loop(1, 64, ask, 0)
    asked[pl.ds(me, 1)] = ask_out[pl.ds(me, 1)]
    most = pl.ds(0, 63)

    def relay(half):
        waiter(shard.at[half], shard_send.at[half], shard_recv.at[half], here).wait_recv()

        @pl.when(is_relay)
        def _():
            for step in (4, 2):
                send(
                    shard.at[half], shard.at[half],
                    relay_send.at[half], shard_recv.at[half], on_line(z + outward * step),
                )

    relay(0)
    waiter(asked.at[most], ask_send, ask_recv, here).wait_recv()
    wanted = asked[...].reshape(512, 128).astype(I32)
    wanted = jnp.concatenate([wanted, wanted], axis=1)
    chosen[...] = onehot(wanted == iota((512, 256), 1) + 1)
    for half in range(2):
        if half:
            relay(half)
        picked = dot(chosen[...], shard[half])
        reply_out[half] = to_blocks(picked[:, 0:128], picked[:, 128:256])

        def answer(step, carry, half=half):
            rank = rem(me + step, 64)
            send(
                reply_out.at[half, rank], replies.at[half, me],
                reply_send.at[half], reply_recv.at[half], member(rank, a),
            )
            return carry

        lax.fori_loop(1, 64, answer, 0)
        replies[half, pl.ds(me, 1)] = reply_out[half, pl.ds(me, 1)]

    loads[2].wait()
    weight = weights_of_pairs(lengths)
    spots = iota((128, 1024), 1)
    finds = (onehot(spots == slot_t), onehot(spots == slot_t + 8))
    parts = []
    for half in range(2):
        waiter(replies.at[half, most], reply_send.at[half], reply_recv.at[half], here).wait_recv()
        arrived = replies[half].reshape(1024, 128)
        parts += [dot(finds[0], arrived), dot(finds[1], arrived)]
    embedded = jnp.concatenate(parts, axis=1)
    center = embedded - mean_rows(embedded)
    embed_scale = lax.rsqrt(mean_rows(center * center) + EPS)
    embed_norm = center * embed_scale
    normed = embed_norm.astype(BF16)

    loads[3].wait()
    for part in range(4):
        cols = pl.ds(512 * part, 512)
        value = dot(normed, w_uvqk[:, cols])
        pre[:, cols] = value
        act[:, cols] = (value * jax.nn.sigmoid(value)).astype(BF16)

    first_half = iota((128, 128), 1) < 64
    keep = (first_half, jnp.logical_not(first_half))
    zero = jnp.zeros((128, 128), BF16)
    mixed = []
    for pair in range(4):
        q = act[:, 1024 + 128 * pair : 1152 + 128 * pair]
        k = act[:, 1536 + 128 * pair : 1664 + 128 * pair]
        v = act[:, 512 + 128 * pair : 640 + 128 * pair]
        both = jnp.zeros((128, 128), F32)
        for head in range(2):
            score = dot(jnp.where(keep[head], q, zero), k, ((1,), (1,))) * 0.125
            attention = (score * jax.nn.sigmoid(score) * weight).astype(BF16)
            both = both + dot(attention, jnp.where(keep[head], v, zero))
        mixed.append(both)
    mixture = jnp.concatenate(mixed, axis=1)
    center = mixture - mean_rows(mixture)
    mix_scale = lax.rsqrt(mean_rows(center * center) + EPS)
    mix_norm = center * mix_scale
    gate = act[:, 0:512].astype(F32)
    gated = (mix_norm * gate).astype(BF16)

    loads[4].wait()
    loads[5].wait()
    cot = cotangent[...]
    grad_o = dot(cot, gated, ((0,), (0,))).astype(BF16)
    for part in range(4):
        for side in range(2):
            grads[part, side, 256:320] = grad_o[128 * part + 64 * side : 128 * part + 64 * side + 64]

    partner = (wide, 2 * y + 1 - c)

    def back(part, grad_normed):
        cols = pl.ds(512 * part, 512)
        value = pre[:, cols]
        gain = jax.nn.sigmoid(value)
        grad_pre = (grad_act[:, cols] * (gain * (1.0 + value * (1.0 - gain)))).astype(BF16)
        grad_u = dot(grad_pre, normed, ((0,), (0,))).astype(BF16)
        for side in range(2):
            grads[part, side, 0:256] = grad_u[256 * side : 256 * side + 256]
        send(grads.at[part, 1 - c], pair_in.at[part], pair_send.at[part], pair_recv.at[part], partner)
        return grad_normed + dot(grad_pre, w_uvqk[:, cols], ((1,), (1,)))

    grad_gated = dot(cot, w_out[...], ((1,), (1,)))
    grad_act[:, 0:512] = grad_gated * mix_norm
    grad_normed = back(0, jnp.zeros((128, 512), F32))
    grad_mix = norm_back(grad_gated * gate, mix_norm, mix_scale).astype(BF16)
    for pair in range(4):
        q = act[:, 1024 + 128 * pair : 1152 + 128 * pair]
        k = act[:, 1536 + 128 * pair : 1664 + 128 * pair]
        v = act[:, 512 + 128 * pair : 640 + 128 * pair]
        g = grad_mix[:, 128 * pair : 128 * pair + 128]
        grad_q, grad_k, grad_v = [jnp.zeros((128, 128), F32)] * 3
        for head in range(2):
            q_one, k_one, v_one, g_one = [jnp.where(keep[head], part, zero) for part in (q, k, v, g)]
            score = dot(q_one, k, ((1,), (1,))) * 0.125
            gain = jax.nn.sigmoid(score)
            attention = (score * gain * weight).astype(BF16)
            grad_att = dot(g_one, v, ((1,), (1,)))
            grad_score = (grad_att * weight * (gain * (1.0 + score * (1.0 - gain))) * 0.125).astype(BF16)
            grad_v = grad_v + dot(attention, g_one, ((0,), (0,)))
            grad_q = grad_q + dot(grad_score, k_one)
            grad_k = grad_k + dot(grad_score, q_one, ((0,), (0,)))
        grad_act[:, 512 + 128 * pair : 640 + 128 * pair] = grad_v
        grad_act[:, 1024 + 128 * pair : 1152 + 128 * pair] = grad_q
        grad_act[:, 1536 + 128 * pair : 1664 + 128 * pair] = grad_k
    for part in range(1, 4):
        grad_normed = back(part, grad_normed)
    grad_embed = (cot.astype(F32) + norm_back(grad_normed, embed_norm, embed_scale)).astype(BF16)

    def give_rows(half):
        given = dot(slots, grad_embed[:, 256 * half : 256 * half + 256])
        rows_out[half] = to_blocks(given[:, 0:128], given[:, 128:256])

        def give(step, carry):
            rank = rem(me + step, 64)
            send(
                rows_out.at[half, rank], rows_in.at[half, me],
                rows_send.at[half], rows_recv.at[half], member(rank, a),
            )
            return carry

        lax.fori_loop(1, 64, give, 0)
        rows_in[half, pl.ds(me, 1)] = rows_out[half, pl.ds(me, 1)]

    give_rows(0)
    for part in range(4):
        waiter(pair_in.at[part], pair_send.at[part], pair_recv.at[part], here).wait()
        mine = grads[part, pl.ds(c, 1)].reshape(320, 512).astype(F32)
        plane_out[part] = (mine + pair_in[part].astype(F32)).astype(BF16)
    for step in range(1, 4):
        to_x, to_y = rem(x + step, 4), rem(y + step, 4)
        send(
            plane_out.at[to_x, pl.ds(0, 160)], x_in.at[x], plane_send.at[0], plane_recv.at[0],
            (to_x * 16 + z, narrow),
        )
        send(
            plane_out.at[:, pl.ds(160, 160), pl.ds(pl.multiple_of(128 * to_y, 128), 128)], y_in.at[y],
            plane_send.at[1], plane_recv.at[1], (wide, 2 * to_y + c),
        )
    my_lanes = pl.ds(pl.multiple_of(128 * y, 128), 128)
    x_in[pl.ds(x, 1)] = plane_out[pl.ds(x, 1), 0:160]
    y_in[pl.ds(y, 1)] = plane_out[:, 160:320, my_lanes].reshape(1, 4, 160, 128)
    give_rows(1)

    for half in range(2):
        waiter(rows_in.at[half, most], rows_send.at[half], rows_recv.at[half], here).wait()
        sums = dot(chosen[...], from_blocks(rows_in[half]), ((0,), (0,))).astype(BF16)
        for piece in range(8):
            piece_out[half, piece] = sums[32 * piece : 32 * piece + 32]

        def give_piece(step, carry, half=half):
            to = rem(narrow + step, 8)
            send(
                piece_out.at[half, to], piece_in.at[half, a],
                piece_send.at[half], piece_recv.at[half], (x * 16 + my_z, to),
            )
            return carry

        lax.fori_loop(0, 8, give_piece, 0)

    three = pl.ds(0, 3)

    def add_up(ref):
        total = ref[0].astype(F32)
        for step in range(1, ref.shape[0]):
            total = total + ref[step].astype(F32)
        return total

    waiter(x_in.at[three], plane_send.at[0], plane_recv.at[0], here).wait()
    x_mid[...] = add_up(x_in).astype(BF16)
    for step in range(1, 4):
        to_y = rem(y + step, 4)
        send(
            x_mid.at[:, pl.ds(pl.multiple_of(128 * to_y, 128), 128)], xy_in.at[y],
            plane_send.at[2], plane_recv.at[2], (wide, 2 * to_y + c),
        )
    xy_in[pl.ds(y, 1)] = x_mid[:, my_lanes].reshape(1, 160, 128)
    waiter(y_in.at[three], plane_send.at[1], plane_recv.at[1], here).wait()
    y_mid[...] = add_up(y_in).astype(BF16)
    for step in range(1, 4):
        to_x = rem(x + step, 4)
        send(y_mid.at[to_x], yx_in.at[x], plane_send.at[3], plane_recv.at[3], (to_x * 16 + z, narrow))
    yx_in[pl.ds(x, 1)] = y_mid[pl.ds(x, 1)]
    waiter(xy_in.at[three], plane_send.at[2], plane_recv.at[2], here).wait()
    waiter(yx_in.at[three], plane_send.at[3], plane_recv.at[3], here).wait()
    total = jnp.concatenate([add_up(xy_in), add_up(yx_in)], axis=0)
    for step in range(8):
        line_out[step] = jnp.concatenate(
            [total[32 * step : 32 * step + 32], total[256 + 8 * step : 264 + 8 * step], jnp.zeros((8, 128), F32)], axis=0
        ).astype(BF16)

    def give_line(step, carry):
        to_z = 8 * c + step
        for core in range(2):
            own = jnp.logical_and(to_z == z, c == core)

            @pl.when(jnp.logical_not(own))
            def _():
                send(line_out.at[step], line_in.at[z], line_send, line_recv, (x * 16 + to_z, 2 * y + core))

            @pl.when(own)
            def _():
                line_in[pl.ds(z, 1)] = line_out[pl.ds(step, 1)]

        return carry

    lax.fori_loop(0, 8, give_line, 0)

    for half in range(2):
        waiter(piece_in.at[half], piece_send.at[half], piece_recv.at[half], here).wait()
        share[half, pl.ds(narrow, 1)] = add_up(piece_in.at[half]).astype(BF16).reshape(1, 32, 256)

        def give_share(step, carry, half=half):
            send(
                share.at[half, narrow], share.at[half, narrow],
                share_send.at[half], share_recv.at[half], (wide, rem(narrow + step, 8)),
            )
            return carry

        lax.fori_loop(1, 8, give_share, 0)

    @pl.when(in_half == 1)
    def _():
        waiter(line_in.at[pl.ds(0, 15)], line_send, line_recv, here).wait()

    @pl.when(in_half == 0)
    def _():
        waiter(line_in, line_send, line_recv, here).wait()

    turned[...] = jnp.concatenate([add_up(line_in), jnp.zeros((80, 128), F32)], axis=0).T
    mine = turned[pl.ds(pl.multiple_of(64 * c, 64), 64), :]
    out_u[...] = mine[:, 0:32]
    out_o[...] = mine[:, 32:40]

    for half in range(2):
        waiter(share.at[half, pl.ds(0, 7)], share_send.at[half], share_recv.at[half], here).wait()
        for piece in range(8):
            out_table[32 * piece : 32 * piece + 32, 256 * half : 256 * half + 256] = share[half, piece].astype(F32)

    waiter(asked.at[most], ask_send, ask_recv, here).wait_send()
    for half in range(2):
        waiter(replies.at[half, most], reply_send.at[half], reply_recv.at[half], here).wait_send()

        @pl.when(is_source)
        def _(half=half):
            for step in range(4):
                waiter(shard.at[half], shard_send.at[half], shard_recv.at[half], here).wait_send()

        @pl.when(is_relay)
        def _(half=half):
            for step in range(2):
                waiter(shard.at[half], relay_send.at[half], shard_recv.at[half], here).wait_send()


def on_device(table, item_owner, item_row, lengths, cotangent, w_uvqk, w_out):
    vmem = pl.BlockSpec(memory_space=pltpu.VMEM)
    anywhere = pl.BlockSpec(memory_space=pl.ANY)
    dma = pltpu.SemaphoreType.DMA
    shape = jax.ShapeDtypeStruct

    def held(*sizes, kind=BF16):
        return pltpu.VMEM(sizes, kind)

    return pl.pallas_call(
        layer_kernel,
        out_shape=(shape((256, 512), F32), shape((64, 32), F32), shape((64, 8), F32)),
        in_specs=[anywhere] * 7,
        out_specs=(vmem,) * 3,
        scratch_shapes=[
            held(1, 128, kind=I32), held(1, 128, kind=I32), held(1, 6, kind=I32),
            held(128, 512), held(512, 2048), held(512, 512),
            held(2, 256, 256), held(64, 8, 128, kind=F32), held(64, 8, 128, kind=F32), held(512, 256),
            held(2, 64, 16, 128), held(2, 64, 16, 128),
            held(128, 2048, kind=F32), held(128, 2048), held(128, 2048, kind=F32),
            held(4, 2, 320, 512), held(2, 64, 16, 128), held(2, 64, 16, 128),
            held(4, 320, 512), held(4, 320, 512),
            held(4, 160, 512), held(4, 4, 160, 128), held(160, 512), held(4, 160, 128),
            held(4, 160, 128), held(4, 160, 128),
            held(8, 48, 128), held(16, 48, 128), held(2, 8, 32, 256), held(2, 8, 32, 256), held(2, 8, 32, 256),
            held(128, 128, kind=F32),
            dma((6,)), dma((2,)), dma((2,)), dma((2,)), dma, dma, dma((2,)), dma((2,)),
            dma((2,)), dma((2,)), dma((4,)), dma((4,)), dma((4,)), dma((4,)), dma, dma,
            dma((2,)), dma((2,)), dma((2,)), dma((2,)),
        ],
        compiler_params=pltpu.CompilerParams(collective_id=0, has_side_effects=True, vmem_limit_bytes=VMEM_LIMIT),
        name="layer",
    )(item_owner.reshape(1, 128), item_row.reshape(1, 128), lengths, table, cotangent, w_uvqk, w_out)


def solution(mesh):
    in_specs = (
        P("wide", None),
        P(("wide", "narrow"), None),
        P(("wide", "narrow")),
        P(("wide", "narrow"), None),
        P(("wide", "narrow"), None),
        P(),
        P(),
    )
    out_specs = (P("wide", None), P("narrow", "wide"), P("narrow", "wide"))
    return jax.shard_map(on_device, mesh=mesh, in_specs=in_specs, out_specs=out_specs, check_vma=False)
```

time: 951 us -> 101 us (0.11); the launches traced: 940 us -> 101 us
  waiting for transfers between devices: 613 us -> 0 us
  blocking collectives: 256 us -> 0 us
  Pallas kernels: 0 us -> 95.6 us
  matrix products: 15.4 us -> 0 us
  starting transfers between devices: 14.7 us -> 0 us
  between operations: 14.8 us -> 0.64 us
  other arithmetic: 14 us -> 0 us
    unnamed x5 -> x0, waiting for transfers between devices: 537 us -> none
    unnamed x1 -> x0, blocking collectives: 224 us -> none
    pallas_call x0 -> x1, Pallas kernels: none -> 95.6 us  [on_device(): pl.pallas_call(layer_kernel, out_shape=(shape((256, 512), F32), shape((64...]
    all_to_all x2 -> x0, waiting for transfers between devices: 51.6 us -> none  [the longest x1 27.5 us: on_device(): lax.all_to_all(picked, 'wide', split_axis=0, concat_axis=0, tiled=True)]
    all_to_all x1 -> x0, blocking collectives: 32.2 us -> none  [on_device(): lax.all_to_all(requests, 'wide', split_axis=0, concat_axis=0, tiled=True)]
    reduce_scatter x2 -> x0, waiting for transfers between devices: 24.9 us -> none  [the longest x1 24.9 us: on_device(): lax.psum_scatter(grad_second.astype(jnp.float32).astype(jnp.bfloat16), 'n...]
    dot_general x12 -> x0, matrix products: 15.4 us -> none  [the longest x3 7.16 us: local_forward(): jnp.dot(normed, w_uvqk, preferred_element_type=jnp.float32)]
    all_to_all x2 -> x0, starting transfers between devices: 14.3 us -> none  [the longest x1 9.71 us: on_device(): lax.all_to_all(outgoing.astype(jnp.bfloat16), 'wide', split_axis=0, conca...]
  transfers between devices with their start and end apart: 6 -> 0, of which waited for: 4 -> 0; matrix products, arithmetic and copies ran while one was open for 2% -> 0% of each run, Pallas kernels for 0% -> 0%
where the time goes in v2:
time: 101 us
  Pallas kernels  95.6 us (95%)
  local copies, waits for them, and re-layouts  4.72 us (5%)
    pallas_call x1, Pallas kernels, on_device(): pl.pallas_call(layer_kernel, out_shape=(shape((256, 512), F32), shape((64...  95.6 us
    pallas_call x2, local copies, waits for them, and re-layouts, on_device(): pl.pallas_call(layer_kernel, out_shape=(shape((256, 512), F32), shape((64...  2.86 us

profile of v2, /device:TPU:1, one launch (start us, length us, event | category | flops | bytes accessed | tf_op | source)
XLA Modules:
  0.0 101.0 jit_solution(5406033671610739576)
XLA Ops:
  0.6 95.6 %layer.1 = (f32[256,512]{1,0:T(8,128)}, f32[64,32]{1,0:T(8,128)}, f32[64,8]{1,0:T(8,128)}) custom-call(s32[1,128]{1,0:T(1,128)} %bitcast.2, s32[1,128]{1,0:T(1,128)} %bitcast.3, s32[1,6]{1,0:T(1,128)} %lengths_hbm.1, bf16[256,512]{1,0:T(8,128)(2,1)} %table.1, bf16[128,512]{1,0:T(8,128)(2,1)} %cotangent_hbm.1, bf16[512,2048]{1,0:T(8,128)(2,1)} %w_uvqk_hbm.1, ...), custom_call_target="tpu_custom_call" | custom-call | tf_op jit(solution)/shard_map/layer/pallas_call | solution.py:482
  96.3 1.4 %copy.11 = f32[64,8]{0,1:T(8,128)} copy(f32[64,8]{1,0:T(8,128)} %get-tuple-element.5) | data formatting | bytes 4096 | tf_op jit(solution)/shard_map/layer/pallas_call | solution.py:482
  97.7 1.4 %copy.10 = f32[64,32]{0,1:T(8,128)} copy(f32[64,32]{1,0:T(8,128)} %get-tuple-element.4) | data formatting | bytes 16384 | tf_op jit(solution)/shard_map/layer/pallas_call | solution.py:482
  99.1 1.9 %copy.13 = f32[256,512]{1,0:T(8,128)} copy(f32[256,512]{1,0:T(8,128)} %get-tuple-element.9) | data formatting | bytes 1048576

commit v3 on v2

--- a/solution.py
+++ b/solution.py
@@ -109,13 +109,13 @@
 
 
 def layer_kernel(
-    owner_hbm, row_hbm, lengths_hbm, table, cotangent_hbm, w_uvqk_hbm, w_out_hbm, out_table, out_u, out_o,
+    owner_hbm, row_hbm, lengths_hbm, table, cotangent_hbm, w_uvqk_hbm, w_out_hbm, shared, out_w,
     owner, row, lengths, cotangent, w_uvqk, w_out, shard, ask_out, asked, chosen, reply_out, replies,
-    pre, act, grad_act, grads, rows_out, rows_in, pair_in, plane_out, x_in, y_in, x_mid, y_mid, xy_in, yx_in,
-    line_out, line_in, piece_out, piece_in, share, turned,
+    pre, act, grad_act, grad_pre, grads, rows_out, rows_in, pair_in, plane_out, x_in, y_in, x_mid, y_mid, xy_in, yx_in,
+    line_out, line_in, sums, far_in, piece_out, piece_in, share,
     load_sem, shard_send, shard_recv, relay_send, ask_send, ask_recv, reply_send, reply_recv,
     rows_send, rows_recv, pair_send, pair_recv, plane_send, plane_recv, line_send, line_recv,
-    piece_send, piece_recv, share_send, share_recv,
+    far_send, far_recv, piece_send, piece_recv, share_send, share_recv, keep_sem,
 ):
     x, z, y, c = coordinates()
     wide = x * 16 + z
@@ -148,21 +148,6 @@
     )
     signal(barrier, on_line(parent))
 
-    def greet_line(step, carry):
-        signal(barrier, (x * 16 + 2 * step + to_b, to_narrow))
-        return carry
-
-    lax.fori_loop(0, 8, greet_line, 0)
-
-    def greet_column(step, carry):
-        @pl.when(jnp.logical_or(step != z, upper != c))
-        def _():
-            signal(barrier, (x * 16 + step, 2 * y + upper))
-
-        return carry
-
-    lax.fori_loop(0, 16, greet_column, 0)
-
     def greet(step, carry):
         signal(barrier, member(rem(me + step, 64), a))
         return carry
@@ -180,17 +165,17 @@
     named = (jnp.broadcast_to(row[...].astype(F32), (128, 128)).T + 1.0).astype(BF16)
     ask_out[...] = dot(slots, named).reshape(64, 8, 128)
 
-    pl.semaphore_wait(barrier, 63 + 8 + 16 - in_half + 4 * is_source.astype(I32) + 2 * is_relay.astype(I32))
-
-    for half in range(2):
-
-        @pl.when(is_source)
-        def _(half=half):
-            for step in (3, -3, 1, -1):
-                send(
-                    table.at[:, pl.ds(256 * half, 256)], shard.at[half],
-                    shard_send.at[half], shard_recv.at[half], on_line(z + step),
-                )
+    pl.semaphore_wait(barrier, 63 + 4 * is_source.astype(I32) + 2 * is_relay.astype(I32))
+
+    @pl.when(is_source)
+    def _():
+        for steps in ((3, -3), (1, -1)):
+            for half in range(2):
+                for step in steps:
+                    send(
+                        table.at[:, pl.ds(256 * half, 256)], shard.at[half],
+                        shard_send.at[half], shard_recv.at[half], on_line(z + step),
+                    )
 
     def ask(step, carry):
         rank = rem(me + step, 64)
@@ -201,25 +186,25 @@
     asked[pl.ds(me, 1)] = ask_out[pl.ds(me, 1)]
     most = pl.ds(0, 63)
 
-    def relay(half):
-        waiter(shard.at[half], shard_send.at[half], shard_recv.at[half], here).wait_recv()
-
-        @pl.when(is_relay)
-        def _():
+    @pl.when(is_relay)
+    def _():
+        for half in range(2):
+            waiter(shard.at[half], shard_send.at[half], shard_recv.at[half], here).wait_recv()
             for step in (4, 2):
                 send(
                     shard.at[half], shard.at[half],
                     relay_send.at[half], shard_recv.at[half], on_line(z + outward * step),
                 )
 
-    relay(0)
     waiter(asked.at[most], ask_send, ask_recv, here).wait_recv()
     wanted = asked[...].reshape(512, 128).astype(I32)
     wanted = jnp.concatenate([wanted, wanted], axis=1)
     chosen[...] = onehot(wanted == iota((512, 256), 1) + 1)
     for half in range(2):
-        if half:
-            relay(half)
+        @pl.when(jnp.logical_not(is_relay))
+        def _(half=half):
+            waiter(shard.at[half], shard_send.at[half], shard_recv.at[half], here).wait_recv()
+
         picked = dot(chosen[...], shard[half])
         reply_out[half] = to_blocks(picked[:, 0:128], picked[:, 128:256])
 
@@ -280,23 +265,13 @@
     loads[4].wait()
     loads[5].wait()
     cot = cotangent[...]
-    grad_o = dot(cot, gated, ((0,), (0,))).astype(BF16)
-    for part in range(4):
-        for side in range(2):
-            grads[part, side, 256:320] = grad_o[128 * part + 64 * side : 128 * part + 64 * side + 64]
-
-    partner = (wide, 2 * y + 1 - c)
 
     def back(part, grad_normed):
         cols = pl.ds(512 * part, 512)
         value = pre[:, cols]
         gain = jax.nn.sigmoid(value)
-        grad_pre = (grad_act[:, cols] * (gain * (1.0 + value * (1.0 - gain)))).astype(BF16)
-        grad_u = dot(grad_pre, normed, ((0,), (0,))).astype(BF16)
-        for side in range(2):
-            grads[part, side, 0:256] = grad_u[256 * side : 256 * side + 256]
-        send(grads.at[part, 1 - c], pair_in.at[part], pair_send.at[part], pair_recv.at[part], partner)
-        return grad_normed + dot(grad_pre, w_uvqk[:, cols], ((1,), (1,)))
+        grad_pre[:, cols] = (grad_act[:, cols] * (gain * (1.0 + value * (1.0 - gain)))).astype(BF16)
+        return grad_normed + dot(grad_pre[:, cols], w_uvqk[:, cols], ((1,), (1,)))
 
     grad_gated = dot(cot, w_out[...], ((1,), (1,)))
     grad_act[:, 0:512] = grad_gated * mix_norm
@@ -341,6 +316,16 @@
         rows_in[half, pl.ds(me, 1)] = rows_out[half, pl.ds(me, 1)]
 
     give_rows(0)
+    give_rows(1)
+
+    grad_o = dot(cot, gated, ((0,), (0,))).astype(BF16)
+    partner = (wide, 2 * y + 1 - c)
+    for part in range(4):
+        grad_u = dot(grad_pre[:, pl.ds(512 * part, 512)], normed, ((0,), (0,))).astype(BF16)
+        for side in range(2):
+            grads[part, side, 0:256] = grad_u[256 * side : 256 * side + 256]
+            grads[part, side, 256:320] = grad_o[128 * part + 64 * side : 128 * part + 64 * side + 64]
+        send(grads.at[part, 1 - c], pair_in.at[part], pair_send.at[part], pair_recv.at[part], partner)
     for part in range(4):
         waiter(pair_in.at[part], pair_send.at[part], pair_recv.at[part], here).wait()
         mine = grads[part, pl.ds(c, 1)].reshape(320, 512).astype(F32)
@@ -358,23 +343,45 @@
     my_lanes = pl.ds(pl.multiple_of(128 * y, 128), 128)
     x_in[pl.ds(x, 1)] = plane_out[pl.ds(x, 1), 0:160]
     y_in[pl.ds(y, 1)] = plane_out[:, 160:320, my_lanes].reshape(1, 4, 160, 128)
-    give_rows(1)
-
-    for half in range(2):
-        waiter(rows_in.at[half, most], rows_send.at[half], rows_recv.at[half], here).wait()
-        sums = dot(chosen[...], from_blocks(rows_in[half]), ((0,), (0,))).astype(BF16)
-        for piece in range(8):
-            piece_out[half, piece] = sums[32 * piece : 32 * piece + 32]
-
-        def give_piece(step, carry, half=half):
+
+    is_far = jnp.logical_and(away >= 5, away <= 11)
+    child = jnp.logical_or(away == 7, away == 9).astype(I32)
+    place = jnp.where(away == 1, 0, jnp.where(away == 3, 1, jnp.where(away == 13, 2, 3)))
+
+    def give_pieces(half):
+        def give(step, carry):
             to = rem(narrow + step, 8)
             send(
-                piece_out.at[half, to], piece_in.at[half, a],
+                piece_out.at[half, pl.ds(pl.multiple_of(32 * to, 32), 32)], piece_in.at[half, place],
                 piece_send.at[half], piece_recv.at[half], (x * 16 + my_z, to),
             )
             return carry
 
-        lax.fori_loop(0, 8, give_piece, 0)
+        lax.fori_loop(0, 8, give, 0)
+
+    for half in range(2):
+        waiter(rows_in.at[half, most], rows_send.at[half], rows_recv.at[half], here).wait()
+        sums[half] = dot(chosen[...], from_blocks(rows_in[half]), ((0,), (0,)))
+
+        @pl.when(jnp.logical_not(is_relay))
+        def _(half=half):
+            piece_out[half] = sums[half].astype(BF16)
+
+            @pl.when(is_far)
+            def _():
+                send(piece_out.at[half], far_in.at[half, child], far_send.at[half], far_recv.at[half], on_line(parent))
+
+            @pl.when(jnp.logical_not(is_far))
+            def _():
+                give_pieces(half)
+
+    @pl.when(is_relay)
+    def _():
+        for half in range(2):
+            waiter(far_in.at[half], far_send.at[half], far_recv.at[half], here).wait_recv()
+            total = sums[half] + far_in[half, 0].astype(F32) + far_in[half, 1].astype(F32)
+            piece_out[half] = total.astype(BF16)
+            give_pieces(half)
 
     three = pl.ds(0, 3)
 
@@ -424,13 +431,16 @@
 
     lax.fori_loop(0, 8, give_line, 0)
 
-    for half in range(2):
-        waiter(piece_in.at[half], piece_send.at[half], piece_recv.at[half], here).wait()
-        share[half, pl.ds(narrow, 1)] = add_up(piece_in.at[half]).astype(BF16).reshape(1, 32, 256)
+    keeps = []
+    for half in range(2):
+        waiter(piece_in.at[half], piece_send.at[half], piece_recv.at[half], here).wait_recv()
+        share[half] = add_up(piece_in.at[half]).astype(BF16)
+        keeps.append(pltpu.make_async_copy(share.at[half], shared.at[half, narrow], keep_sem.at[half]))
+        keeps[-1].start()
 
         def give_share(step, carry, half=half):
             send(
-                share.at[half, narrow], share.at[half, narrow],
+                share.at[half], shared.at[half, narrow],
                 share_send.at[half], share_recv.at[half], (wide, rem(narrow + step, 8)),
             )
             return carry
@@ -445,15 +455,8 @@
     def _():
         waiter(line_in, line_send, line_recv, here).wait()
 
-    turned[...] = jnp.concatenate([add_up(line_in), jnp.zeros((80, 128), F32)], axis=0).T
-    mine = turned[pl.ds(pl.multiple_of(64 * c, 64), 64), :]
-    out_u[...] = mine[:, 0:32]
-    out_o[...] = mine[:, 32:40]
-
-    for half in range(2):
-        waiter(share.at[half, pl.ds(0, 7)], share_send.at[half], share_recv.at[half], here).wait()
-        for piece in range(8):
-            out_table[32 * piece : 32 * piece + 32, 256 * half : 256 * half + 256] = share[half, piece].astype(F32)
+    total = add_up(line_in)
+    out_w[...] = jnp.where(c == 0, total[0:40, 0:64], total[0:40, 64:128])
 
     waiter(asked.at[most], ask_send, ask_recv, here).wait_send()
     for half in range(2):
@@ -468,6 +471,25 @@
         def _(half=half):
             for step in range(2):
                 waiter(shard.at[half], relay_send.at[half], shard_recv.at[half], here).wait_send()
+
+        @pl.when(is_far)
+        def _(half=half):
+            waiter(piece_out.at[half], far_send.at[half], far_recv.at[half], here).wait_send()
+
+        @pl.when(jnp.logical_not(is_far))
+        def _(half=half):
+            waiter(piece_out.at[half], piece_send.at[half], piece_recv.at[half], here).wait_send()
+
+    for half in range(2):
+        waiter(shared.at[half, pl.ds(0, 7)], share_send.at[half], share_recv.at[half], here).wait()
+        keeps[half].wait()
+
+
+def finish_kernel(shared, sums, out_table, out_u, out_o):
+    for half in range(2):
+        out_table[:, 256 * half : 256 * half + 256] = shared[half].reshape(256, 256).astype(F32)
+    out_u[...] = sums[0:32]
+    out_o[...] = sums[32:40]
 
 
 def on_device(table, item_owner, item_row, lengths, cotangent, w_uvqk, w_out):
@@ -479,30 +501,39 @@
     def held(*sizes, kind=BF16):
         return pltpu.VMEM(sizes, kind)
 
-    return pl.pallas_call(
+    shared, sums = pl.pallas_call(
         layer_kernel,
-        out_shape=(shape((256, 512), F32), shape((64, 32), F32), shape((64, 8), F32)),
+        out_shape=(shape((2, 8, 32, 256), BF16), shape((40, 64), F32)),
         in_specs=[anywhere] * 7,
-        out_specs=(vmem,) * 3,
+        out_specs=(anywhere, vmem),
         scratch_shapes=[
             held(1, 128, kind=I32), held(1, 128, kind=I32), held(1, 6, kind=I32),
             held(128, 512), held(512, 2048), held(512, 512),
             held(2, 256, 256), held(64, 8, 128, kind=F32), held(64, 8, 128, kind=F32), held(512, 256),
             held(2, 64, 16, 128), held(2, 64, 16, 128),
-            held(128, 2048, kind=F32), held(128, 2048), held(128, 2048, kind=F32),
+            held(128, 2048, kind=F32), held(128, 2048), held(128, 2048, kind=F32), held(128, 2048),
             held(4, 2, 320, 512), held(2, 64, 16, 128), held(2, 64, 16, 128),
             held(4, 320, 512), held(4, 320, 512),
             held(4, 160, 512), held(4, 4, 160, 128), held(160, 512), held(4, 160, 128),
             held(4, 160, 128), held(4, 160, 128),
-            held(8, 48, 128), held(16, 48, 128), held(2, 8, 32, 256), held(2, 8, 32, 256), held(2, 8, 32, 256),
-            held(128, 128, kind=F32),
+            held(8, 48, 128), held(16, 48, 128),
+            held(2, 256, 256, kind=F32), held(2, 2, 256, 256), held(2, 256, 256), held(2, 4, 32, 256), held(2, 32, 256),
             dma((6,)), dma((2,)), dma((2,)), dma((2,)), dma, dma, dma((2,)), dma((2,)),
             dma((2,)), dma((2,)), dma((4,)), dma((4,)), dma((4,)), dma((4,)), dma, dma,
-            dma((2,)), dma((2,)), dma((2,)), dma((2,)),
+            dma((2,)), dma((2,)), dma((2,)), dma((2,)), dma((2,)), dma((2,)), dma((2,)),
         ],
         compiler_params=pltpu.CompilerParams(collective_id=0, has_side_effects=True, vmem_limit_bytes=VMEM_LIMIT),
         name="layer",
     )(item_owner.reshape(1, 128), item_row.reshape(1, 128), lengths, table, cotangent, w_uvqk, w_out)
+
+    grad_table, grad_uvqk, grad_out = pl.pallas_call(
+        finish_kernel,
+        out_shape=(shape((256, 512), F32), shape((32, 64), F32), shape((8, 64), F32)),
+        in_specs=[vmem] * 2,
+        out_specs=(vmem,) * 3,
+        name="finish",
+    )(shared, sums)
+    return grad_table, grad_uvqk.T, grad_out.T
 
 
 def solution(mesh):

time: 101 us -> 86.8 us (0.86)
  Pallas kernels: 95.6 us -> 85.7 us
  local copies, waits for them, and re-layouts: 4.72 us -> 0 us
    pallas_call x1 -> x2, Pallas kernels: 95.6 us -> 85.7 us  [the longest x1 83.9 us: on_device(): pl.pallas_call(layer_kernel, out_shape=(shape((2, 8, 32, 256), BF16), sha...]
    pallas_call x2 -> x0, local copies, waits for them, and re-layouts: 2.86 us -> none  [on_device(): pl.pallas_call(layer_kernel, out_shape=(shape((256, 512), F32), shape((64...]
    unnamed x1 -> x0, local copies, waits for them, and re-layouts: 1.87 us -> none
where the time goes in v3:
time: 86.8 us; the launch traced here: 86.3 us
  Pallas kernels  85.7 us (99%)
    pallas_call x1, Pallas kernels, on_device(): pl.pallas_call(layer_kernel, out_shape=(shape((2, 8, 32, 256), BF16), sha...  83.9 us
    pallas_call x1, Pallas kernels, on_device(): pl.pallas_call(finish_kernel, out_shape=(shape((256, 512), F32), shape((3...  1.79 us

profile of v3, /device:TPU:1, one launch (start us, length us, event | category | flops | bytes accessed | tf_op | source)
XLA Modules:
  0.0 86.3 jit_solution(6991163169631467425)
XLA Ops:
  0.6 83.9 %layer.1 = (bf16[2,8,32,256]{3,2,1,0:T(8,128)(2,1)}, f32[40,64]{1,0:T(8,128)}) custom-call(s32[1,128]{1,0:T(1,128)} %bitcast.4, s32[1,128]{1,0:T(1,128)} %bitcast.5, s32[1,6]{1,0:T(1,128)} %lengths_hbm.1, bf16[256,512]{1,0:T(8,128)(2,1)} %table.1, bf16[128,512]{1,0:T(8,128)(2,1)} %cotangent_hbm.1, bf16[512,2048]{1,0:T(8,128)(2,1)} %w_uvqk_hbm.1, ...), custom_call_target="tpu_custom_call" | custom-call | tf_op jit(solution)/shard_map/layer/pallas_call | solution.py:504
  84.5 1.8 %finish.1 = (f32[256,512]{1,0:T(8,128)}, f32[32,64]{1,0:T(8,128)}, f32[8,64]{1,0:T(8,128)}) custom-call(bf16[2,8,32,256]{3,2,1,0:T(8,128)(2,1)} %get-tuple-element.8.shared, f32[40,64]{1,0:T(8,128)} %get-tuple-element.9.sums), custom_call_target="tpu_custom_call" | custom-call | tf_op jit(solution)/shard_map/finish/pallas_call | solution.py:529

commit v4 on v3

--- a/solution.py
+++ b/solution.py
@@ -77,13 +77,8 @@
     return down, across
 
 
-def to_blocks(first, second):
-    return jnp.concatenate([first.reshape(64, 8, 128), second.reshape(64, 8, 128)], axis=1).astype(BF16)
-
-
-def from_blocks(blocks):
-    values = blocks.astype(F32)
-    return jnp.concatenate([values[:, 0:8].reshape(512, 128), values[:, 8:16].reshape(512, 128)], axis=1).astype(BF16)
+def to_blocks(first, second, lanes):
+    return jnp.concatenate([first.reshape(64, 8, lanes), second.reshape(64, 8, lanes)], axis=1).astype(BF16)
 
 
 def mean_rows(values):
@@ -112,10 +107,10 @@
     owner_hbm, row_hbm, lengths_hbm, table, cotangent_hbm, w_uvqk_hbm, w_out_hbm, shared, out_w,
     owner, row, lengths, cotangent, w_uvqk, w_out, shard, ask_out, asked, chosen, reply_out, replies,
     pre, act, grad_act, grad_pre, grads, rows_out, rows_in, pair_in, plane_out, x_in, y_in, x_mid, y_mid, xy_in, yx_in,
-    line_out, line_in, sums, far_in, piece_out, piece_in, share,
-    load_sem, shard_send, shard_recv, relay_send, ask_send, ask_recv, reply_send, reply_recv,
+    line_out, line_in, sums, chain_in, chain_out, piece_in, share,
+    load_sem, shard_send, shard_recv, pass_send, ask_send, ask_recv, reply_send, reply_recv,
     rows_send, rows_recv, pair_send, pair_recv, plane_send, plane_recv, line_send, line_recv,
-    far_send, far_recv, piece_send, piece_recv, share_send, share_recv, keep_sem,
+    chain_send, chain_recv, piece_recv, share_send, share_recv, keep_sem,
 ):
     x, z, y, c = coordinates()
     wide = x * 16 + z
@@ -127,8 +122,9 @@
     to_narrow, to_b = holder_of(z)
     is_source = to_narrow == narrow
     away = rem(z - my_z + 16, 16)
-    is_relay = jnp.logical_or(away == 3, away == 13)
-    outward = jnp.where(away == 3, 1, -1)
+    outward = jnp.where(away < 8, 1, -1)
+    hops = jnp.where(away < 8, away, 16 - away)
+    passes_on = hops < 7
     upper = div(z, 8)
     in_half = (upper == c).astype(I32)
     barrier = pltpu.get_barrier_semaphore()
@@ -143,9 +139,7 @@
         loads.append(pltpu.make_async_copy(src, dst, load_sem.at[i]))
         loads[-1].start()
 
-    parent = jnp.where(
-        jnp.logical_or(away == 5, away == 7), my_z + 3, jnp.where(jnp.logical_or(away == 9, away == 11), my_z - 3, my_z)
-    )
+    parent = jnp.where(hops == 1, my_z, z - 2 * outward)
     signal(barrier, on_line(parent))
 
     def greet(step, carry):
@@ -165,17 +159,16 @@
     named = (jnp.broadcast_to(row[...].astype(F32), (128, 128)).T + 1.0).astype(BF16)
     ask_out[...] = dot(slots, named).reshape(64, 8, 128)
 
-    pl.semaphore_wait(barrier, 63 + 4 * is_source.astype(I32) + 2 * is_relay.astype(I32))
+    pl.semaphore_wait(barrier, 63 + 2 * is_source.astype(I32) + passes_on.astype(I32))
 
     @pl.when(is_source)
     def _():
-        for steps in ((3, -3), (1, -1)):
-            for half in range(2):
-                for step in steps:
-                    send(
-                        table.at[:, pl.ds(256 * half, 256)], shard.at[half],
-                        shard_send.at[half], shard_recv.at[half], on_line(z + step),
-                    )
+        for piece in range(4):
+            for step in (1, -1):
+                send(
+                    table.at[:, pl.ds(128 * piece, 128)], shard.at[piece],
+                    shard_send.at[piece], shard_recv.at[piece], on_line(z + step),
+                )
 
     def ask(step, carry):
         rank = rem(me + step, 64)
@@ -186,27 +179,27 @@
     asked[pl.ds(me, 1)] = ask_out[pl.ds(me, 1)]
     most = pl.ds(0, 63)
 
-    @pl.when(is_relay)
+    @pl.when(passes_on)
     def _():
-        for half in range(2):
-            waiter(shard.at[half], shard_send.at[half], shard_recv.at[half], here).wait_recv()
-            for step in (4, 2):
-                send(
-                    shard.at[half], shard.at[half],
-                    relay_send.at[half], shard_recv.at[half], on_line(z + outward * step),
-                )
+        for piece in range(4):
+            waiter(shard.at[piece], shard_send.at[piece], shard_recv.at[piece], here).wait_recv()
+            send(
+                shard.at[piece], shard.at[piece],
+                pass_send.at[piece], shard_recv.at[piece], on_line(z + 2 * outward),
+            )
 
     waiter(asked.at[most], ask_send, ask_recv, here).wait_recv()
     wanted = asked[...].reshape(512, 128).astype(I32)
     wanted = jnp.concatenate([wanted, wanted], axis=1)
     chosen[...] = onehot(wanted == iota((512, 256), 1) + 1)
     for half in range(2):
-        @pl.when(jnp.logical_not(is_relay))
+        @pl.when(jnp.logical_not(passes_on))
         def _(half=half):
-            waiter(shard.at[half], shard_send.at[half], shard_recv.at[half], here).wait_recv()
-
-        picked = dot(chosen[...], shard[half])
-        reply_out[half] = to_blocks(picked[:, 0:128], picked[:, 128:256])
+            for piece in (2 * half, 2 * half + 1):
+                waiter(shard.at[piece], shard_send.at[piece], shard_recv.at[piece], here).wait_recv()
+
+        picked = dot(chosen[...], jnp.concatenate([shard[2 * half], shard[2 * half + 1]], axis=1))
+        reply_out[half] = to_blocks(picked[:, 0:128], picked[:, 128:256], 128)
 
         def answer(step, carry, half=half):
             rank = rem(me + step, 64)
@@ -300,23 +293,16 @@
         grad_normed = back(part, grad_normed)
     grad_embed = (cot.astype(F32) + norm_back(grad_normed, embed_norm, embed_scale)).astype(BF16)
 
-    def give_rows(half):
-        given = dot(slots, grad_embed[:, 256 * half : 256 * half + 256])
-        rows_out[half] = to_blocks(given[:, 0:128], given[:, 128:256])
-
-        def give(step, carry):
-            rank = rem(me + step, 64)
-            send(
-                rows_out.at[half, rank], rows_in.at[half, me],
-                rows_send.at[half], rows_recv.at[half], member(rank, a),
-            )
-            return carry
-
-        lax.fori_loop(1, 64, give, 0)
-        rows_in[half, pl.ds(me, 1)] = rows_out[half, pl.ds(me, 1)]
-
-    give_rows(0)
-    give_rows(1)
+    given = dot(slots, grad_embed)
+    rows_out[...] = to_blocks(given[:, 0:256], given[:, 256:512], 256)
+
+    def give_rows(step, carry):
+        rank = rem(me + step, 64)
+        send(rows_out.at[rank], rows_in.at[me], rows_send, rows_recv, member(rank, a))
+        return carry
+
+    lax.fori_loop(1, 64, give_rows, 0)
+    rows_in[pl.ds(me, 1)] = rows_out[pl.ds(me, 1)]
 
     grad_o = dot(cot, gated, ((0,), (0,))).astype(BF16)
     partner = (wide, 2 * y + 1 - c)
@@ -344,44 +330,39 @@
     x_in[pl.ds(x, 1)] = plane_out[pl.ds(x, 1), 0:160]
     y_in[pl.ds(y, 1)] = plane_out[:, 160:320, my_lanes].reshape(1, 4, 160, 128)
 
-    is_far = jnp.logical_and(away >= 5, away <= 11)
-    child = jnp.logical_or(away == 7, away == 9).astype(I32)
-    place = jnp.where(away == 1, 0, jnp.where(away == 3, 1, jnp.where(away == 13, 2, 3)))
-
-    def give_pieces(half):
-        def give(step, carry):
-            to = rem(narrow + step, 8)
-            send(
-                piece_out.at[half, pl.ds(pl.multiple_of(32 * to, 32), 32)], piece_in.at[half, place],
-                piece_send.at[half], piece_recv.at[half], (x * 16 + my_z, to),
-            )
-            return carry
-
-        lax.fori_loop(0, 8, give, 0)
-
-    for half in range(2):
-        waiter(rows_in.at[half, most], rows_send.at[half], rows_recv.at[half], here).wait()
-        sums[half] = dot(chosen[...], from_blocks(rows_in[half]), ((0,), (0,)))
-
-        @pl.when(jnp.logical_not(is_relay))
-        def _(half=half):
-            piece_out[half] = sums[half].astype(BF16)
-
-            @pl.when(is_far)
-            def _():
-                send(piece_out.at[half], far_in.at[half, child], far_send.at[half], far_recv.at[half], on_line(parent))
-
-            @pl.when(jnp.logical_not(is_far))
-            def _():
-                give_pieces(half)
-
-    @pl.when(is_relay)
+    waiter(rows_in.at[most], rows_send, rows_recv, here).wait()
+    arrived = rows_in[...].astype(F32)
+    for half in range(2):
+        sums[half] = dot(chosen[...], arrived[:, 8 * half : 8 * half + 8].reshape(512, 256).astype(BF16), ((0,), (0,)))
+
+    def pass_sums():
+        for piece in range(4):
+            mine = sums[piece // 2, :, 128 * (piece % 2) : 128 * (piece % 2) + 128]
+            chain_out[piece] = mine.astype(BF16)
+
+            @pl.when(passes_on)
+            def _(piece=piece, mine=mine):
+                waiter(chain_in.at[piece], chain_send.at[piece], chain_recv.at[piece], here).wait_recv()
+                chain_out[piece] = (mine + chain_in[piece].astype(F32)).astype(BF16)
+
+            @pl.when(hops > 1)
+            def _(piece=piece):
+                send(
+                    chain_out.at[piece], chain_in.at[piece],
+                    chain_send.at[piece], chain_recv.at[piece], on_line(parent),
+                )
+
+            @pl.when(hops == 1)
+            def _(piece=piece):
+                for to in range(8):
+                    send(
+                        chain_out.at[piece, pl.ds(32 * to, 32)], piece_in.at[piece, div(1 - outward, 2)],
+                        chain_send.at[piece], piece_recv.at[piece], (x * 16 + my_z, to),
+                    )
+
+    @pl.when(hops > 1)
     def _():
-        for half in range(2):
-            waiter(far_in.at[half], far_send.at[half], far_recv.at[half], here).wait_recv()
-            total = sums[half] + far_in[half, 0].astype(F32) + far_in[half, 1].astype(F32)
-            piece_out[half] = total.astype(BF16)
-            give_pieces(half)
+        pass_sums()
 
     three = pl.ds(0, 3)
 
@@ -406,13 +387,22 @@
         to_x = rem(x + step, 4)
         send(y_mid.at[to_x], yx_in.at[x], plane_send.at[3], plane_recv.at[3], (to_x * 16 + z, narrow))
     yx_in[pl.ds(x, 1)] = y_mid[pl.ds(x, 1)]
+    @pl.when(hops == 1)
+    def _():
+        pass_sums()
+
     waiter(xy_in.at[three], plane_send.at[2], plane_recv.at[2], here).wait()
     waiter(yx_in.at[three], plane_send.at[3], plane_recv.at[3], here).wait()
     total = jnp.concatenate([add_up(xy_in), add_up(yx_in)], axis=0)
+    rolled = pltpu.roll(total, 64, 1)
+    left = iota((16, 128), 1) < 64
     for step in range(8):
-        line_out[step] = jnp.concatenate(
-            [total[32 * step : 32 * step + 32], total[256 + 8 * step : 264 + 8 * step], jnp.zeros((8, 128), F32)], axis=0
-        ).astype(BF16)
+        top, bottom = slice(32 * step, 32 * step + 16), slice(32 * step + 16, 32 * step + 32)
+        rest = slice(256 + 8 * step, 264 + 8 * step)
+        first = jnp.where(left, total[top], rolled[bottom])
+        second = jnp.where(left, rolled[top], total[bottom])
+        for core, packed, values in ((0, first, total), (1, second, rolled)):
+            line_out[step, core] = jnp.concatenate([packed, values[rest], jnp.zeros((8, 128), F32)], axis=0).astype(BF16)
 
     def give_line(step, carry):
         to_z = 8 * c + step
@@ -421,11 +411,11 @@
 
             @pl.when(jnp.logical_not(own))
             def _():
-                send(line_out.at[step], line_in.at[z], line_send, line_recv, (x * 16 + to_z, 2 * y + core))
+                send(line_out.at[step, core], line_in.at[z], line_send, line_recv, (x * 16 + to_z, 2 * y + core))
 
             @pl.when(own)
             def _():
-                line_in[pl.ds(z, 1)] = line_out[pl.ds(step, 1)]
+                line_in[pl.ds(z, 1)] = line_out[pl.ds(step, 1), core]
 
         return carry
 
@@ -433,8 +423,11 @@
 
     keeps = []
     for half in range(2):
-        waiter(piece_in.at[half], piece_send.at[half], piece_recv.at[half], here).wait_recv()
-        share[half] = add_up(piece_in.at[half]).astype(BF16)
+        quarters = []
+        for piece in (2 * half, 2 * half + 1):
+            waiter(piece_in.at[piece], chain_send.at[piece], piece_recv.at[piece], here).wait_recv()
+            quarters.append(add_up(piece_in.at[piece]))
+        share[half] = jnp.concatenate(quarters, axis=1).astype(BF16)
         keeps.append(pltpu.make_async_copy(share.at[half], shared.at[half, narrow], keep_sem.at[half]))
         keeps[-1].start()
 
@@ -456,29 +449,26 @@
         waiter(line_in, line_send, line_recv, here).wait()
 
     total = add_up(line_in)
-    out_w[...] = jnp.where(c == 0, total[0:40, 0:64], total[0:40, 64:128])
+    out_w[0:16] = total[0:16, 0:64]
+    out_w[16:32] = total[0:16, 64:128]
+    out_w[32:40] = total[16:24, 0:64]
 
     waiter(asked.at[most], ask_send, ask_recv, here).wait_send()
     for half in range(2):
         waiter(replies.at[half, most], reply_send.at[half], reply_recv.at[half], here).wait_send()
 
+    for piece in range(4):
+
         @pl.when(is_source)
-        def _(half=half):
-            for step in range(4):
-                waiter(shard.at[half], shard_send.at[half], shard_recv.at[half], here).wait_send()
-
-        @pl.when(is_relay)
-        def _(half=half):
+        def _(piece=piece):
             for step in range(2):
-                waiter(shard.at[half], relay_send.at[half], shard_recv.at[half], here).wait_send()
-
-        @pl.when(is_far)
-        def _(half=half):
-            waiter(piece_out.at[half], far_send.at[half], far_recv.at[half], here).wait_send()
-
-        @pl.when(jnp.logical_not(is_far))
-        def _(half=half):
-            waiter(piece_out.at[half], piece_send.at[half], piece_recv.at[half], here).wait_send()
+                waiter(shard.at[piece], shard_send.at[piece], shard_recv.at[piece], here).wait_send()
+
+        @pl.when(passes_on)
+        def _(piece=piece):
+            waiter(shard.at[piece], pass_send.at[piece], shard_recv.at[piece], here).wait_send()
+
+        waiter(chain_out.at[piece], chain_send.at[piece], chain_recv.at[piece], here).wait_send()
 
     for half in range(2):
         waiter(shared.at[half, pl.ds(0, 7)], share_send.at[half], share_recv.at[half], here).wait()
@@ -509,18 +499,18 @@
         scratch_shapes=[
             held(1, 128, kind=I32), held(1, 128, kind=I32), held(1, 6, kind=I32),
             held(128, 512), held(512, 2048), held(512, 512),
-            held(2, 256, 256), held(64, 8, 128, kind=F32), held(64, 8, 128, kind=F32), held(512, 256),
+            held(4, 256, 128), held(64, 8, 128, kind=F32), held(64, 8, 128, kind=F32), held(512, 256),
             held(2, 64, 16, 128), held(2, 64, 16, 128),
             held(128, 2048, kind=F32), held(128, 2048), held(128, 2048, kind=F32), held(128, 2048),
-            held(4, 2, 320, 512), held(2, 64, 16, 128), held(2, 64, 16, 128),
+            held(4, 2, 320, 512), held(64, 16, 256), held(64, 16, 256),
             held(4, 320, 512), held(4, 320, 512),
             held(4, 160, 512), held(4, 4, 160, 128), held(160, 512), held(4, 160, 128),
             held(4, 160, 128), held(4, 160, 128),
-            held(8, 48, 128), held(16, 48, 128),
-            held(2, 256, 256, kind=F32), held(2, 2, 256, 256), held(2, 256, 256), held(2, 4, 32, 256), held(2, 32, 256),
-            dma((6,)), dma((2,)), dma((2,)), dma((2,)), dma, dma, dma((2,)), dma((2,)),
-            dma((2,)), dma((2,)), dma((4,)), dma((4,)), dma((4,)), dma((4,)), dma, dma,
-            dma((2,)), dma((2,)), dma((2,)), dma((2,)), dma((2,)), dma((2,)), dma((2,)),
+            held(8, 2, 32, 128), held(16, 32, 128),
+            held(2, 256, 256, kind=F32), held(4, 256, 128), held(4, 256, 128), held(4, 2, 32, 128), held(2, 32, 256),
+            dma((6,)), dma((4,)), dma((4,)), dma((4,)), dma, dma, dma((2,)), dma((2,)),
+            dma, dma, dma((4,)), dma((4,)), dma((4,)), dma((4,)), dma, dma,
+            dma((4,)), dma((4,)), dma((4,)), dma((2,)), dma((2,)), dma((2,)),
         ],
         compiler_params=pltpu.CompilerParams(collective_id=0, has_side_effects=True, vmem_limit_bytes=VMEM_LIMIT),
         name="layer",

time: 86.8 us -> 88.6 us (1.021)
  Pallas kernels: 85.7 us -> 87.7 us
    pallas_call x1, Pallas kernels: 83.9 us -> 85.9 us  [on_device(): pl.pallas_call(layer_kernel, out_shape=(shape((2, 8, 32, 256), BF16), sha...]
where the time goes in v4:
time: 88.6 us; the launch traced here: 88.3 us
  Pallas kernels  87.7 us (99%)
    pallas_call x1, Pallas kernels, on_device(): pl.pallas_call(layer_kernel, out_shape=(shape((2, 8, 32, 256), BF16), sha...  85.9 us
    pallas_call x1, Pallas kernels, on_device(): pl.pallas_call(finish_kernel, out_shape=(shape((256, 512), F32), shape((3...  1.79 us

profile of v4, /device:TPU:1, one launch (start us, length us, event | category | flops | bytes accessed | tf_op | source)
XLA Modules:
  0.0 88.3 jit_solution(15844634592748503291)
XLA Ops:
  0.6 85.9 %layer.1 = (bf16[2,8,32,256]{3,2,1,0:T(8,128)(2,1)}, f32[40,64]{1,0:T(8,128)}) custom-call(s32[1,128]{1,0:T(1,128)} %bitcast.4, s32[1,128]{1,0:T(1,128)} %bitcast.5, s32[1,6]{1,0:T(1,128)} %lengths_hbm.1, bf16[256,512]{1,0:T(8,128)(2,1)} %table.1, bf16[128,512]{1,0:T(8,128)(2,1)} %cotangent_hbm.1, bf16[512,2048]{1,0:T(8,128)(2,1)} %w_uvqk_hbm.1, ...), custom_call_target="tpu_custom_call" | custom-call | tf_op jit(solution)/shard_map/layer/pallas_call | solution.py:494
  86.6 1.8 %finish.1 = (f32[256,512]{1,0:T(8,128)}, f32[32,64]{1,0:T(8,128)}, f32[8,64]{1,0:T(8,128)}) custom-call(bf16[2,8,32,256]{3,2,1,0:T(8,128)(2,1)} %get-tuple-element.8.shared, f32[40,64]{1,0:T(8,128)} %get-tuple-element.9.sums), custom_call_target="tpu_custom_call" | custom-call | tf_op jit(solution)/shard_map/finish/pallas_call | solution.py:519

commit v5 on v4

--- a/solution.py
+++ b/solution.py
@@ -36,9 +36,12 @@
     return 2 * y + div(half, 4), b
 
 
-def member(rank, a):
-    narrow, b = holder_of(rem(rank, 16))
-    return div(rank, 16) * 16 + 2 * a + b, narrow
+def member(step, x, y, c, a, b):
+    far = (div(step, 16), rem(div(step, 4), 4))
+    dx, dy = [jnp.where(i == 0, 2, jnp.where(i == 1, 1, jnp.where(i == 2, 3, 0))) for i in far]
+    to_x, to_y = rem(x + dx, 4), rem(y + dy, 4)
+    to_b, to_c = rem(b + 1 + rem(div(step, 2), 2), 2), rem(c + 1 + rem(step, 2), 2)
+    return to_x * 16 + shard_z(to_y, to_c, to_b), (to_x * 16 + 2 * a + to_b, 2 * to_y + to_c)
 
 
 def signal(sem, device):
@@ -105,8 +108,8 @@
 
 def layer_kernel(
     owner_hbm, row_hbm, lengths_hbm, table, cotangent_hbm, w_uvqk_hbm, w_out_hbm, shared, out_w,
-    owner, row, lengths, cotangent, w_uvqk, w_out, shard, ask_out, asked, chosen, reply_out, replies,
-    pre, act, grad_act, grad_pre, grads, rows_out, rows_in, pair_in, plane_out, x_in, y_in, x_mid, y_mid, xy_in, yx_in,
+    owner, row, lengths, cotangent, w_uvqk, w_out, own_shard, shard, ask_out, asked, chosen, reply_out, replies,
+    pre, act, grad_act, grad_pre, grads, rows_out, rows_in, pair_in, x_out, y_out, x_in, y_in, x_mid, y_mid, xy_in, yx_in,
     line_out, line_in, sums, chain_in, chain_out, piece_in, share,
     load_sem, shard_send, shard_recv, pass_send, ask_send, ask_recv, reply_send, reply_recv,
     rows_send, rows_recv, pair_send, pair_recv, plane_send, plane_recv, line_send, line_recv,
@@ -124,7 +127,8 @@
     away = rem(z - my_z + 16, 16)
     outward = jnp.where(away < 8, 1, -1)
     hops = jnp.where(away < 8, away, 16 - away)
-    passes_on = hops < 7
+    is_relay = hops == 3
+    is_far = hops > 3
     upper = div(z, 8)
     in_half = (upper == c).astype(I32)
     barrier = pltpu.get_barrier_semaphore()
@@ -135,18 +139,19 @@
     loads = []
     for i, (src, dst) in enumerate(
         [(owner_hbm, owner), (row_hbm, row), (lengths_hbm, lengths), (w_uvqk_hbm, w_uvqk), (cotangent_hbm, cotangent), (w_out_hbm, w_out)]
+        + [(table.at[:, pl.ds(128 * piece, 128)], own_shard.at[piece]) for piece in range(4)]
     ):
         loads.append(pltpu.make_async_copy(src, dst, load_sem.at[i]))
         loads[-1].start()
 
-    parent = jnp.where(hops == 1, my_z, z - 2 * outward)
+    parent = jnp.where(hops > 3, my_z + 3 * outward, my_z)
     signal(barrier, on_line(parent))
 
     def greet(step, carry):
-        signal(barrier, member(rem(me + step, 64), a))
+        signal(barrier, member(step, x, y, c, a, b)[1])
         return carry
 
-    lax.fori_loop(1, 64, greet, 0)
+    lax.fori_loop(0, 63, greet, 0)
 
     loads[0].wait()
     loads[1].wait()
@@ -159,41 +164,44 @@
     named = (jnp.broadcast_to(row[...].astype(F32), (128, 128)).T + 1.0).astype(BF16)
     ask_out[...] = dot(slots, named).reshape(64, 8, 128)
 
-    pl.semaphore_wait(barrier, 63 + 2 * is_source.astype(I32) + passes_on.astype(I32))
+    for piece in range(4):
+        loads[6 + piece].wait()
+    pl.semaphore_wait(barrier, 63 + 4 * is_source.astype(I32) + 2 * is_relay.astype(I32))
 
     @pl.when(is_source)
     def _():
         for piece in range(4):
-            for step in (1, -1):
+            for step in (3, -3, 1, -1):
                 send(
-                    table.at[:, pl.ds(128 * piece, 128)], shard.at[piece],
+                    own_shard.at[piece], shard.at[piece],
                     shard_send.at[piece], shard_recv.at[piece], on_line(z + step),
                 )
 
     def ask(step, carry):
-        rank = rem(me + step, 64)
-        send(ask_out.at[rank], asked.at[me], ask_send, ask_recv, member(rank, a))
+        rank, device = member(step, x, y, c, a, b)
+        send(ask_out.at[rank], asked.at[me], ask_send, ask_recv, device)
         return carry
 
-    lax.fori_loop(1, 64, ask, 0)
+    lax.fori_loop(0, 63, ask, 0)
     asked[pl.ds(me, 1)] = ask_out[pl.ds(me, 1)]
     most = pl.ds(0, 63)
 
-    @pl.when(passes_on)
+    @pl.when(is_relay)
     def _():
         for piece in range(4):
             waiter(shard.at[piece], shard_send.at[piece], shard_recv.at[piece], here).wait_recv()
-            send(
-                shard.at[piece], shard.at[piece],
-                pass_send.at[piece], shard_recv.at[piece], on_line(z + 2 * outward),
-            )
+            for step in (4, 2):
+                send(
+                    shard.at[piece], shard.at[piece],
+                    pass_send.at[piece], shard_recv.at[piece], on_line(z + outward * step),
+                )
 
     waiter(asked.at[most], ask_send, ask_recv, here).wait_recv()
     wanted = asked[...].reshape(512, 128).astype(I32)
     wanted = jnp.concatenate([wanted, wanted], axis=1)
     chosen[...] = onehot(wanted == iota((512, 256), 1) + 1)
     for half in range(2):
-        @pl.when(jnp.logical_not(passes_on))
+        @pl.when(jnp.logical_not(is_relay))
         def _(half=half):
             for piece in (2 * half, 2 * half + 1):
                 waiter(shard.at[piece], shard_send.at[piece], shard_recv.at[piece], here).wait_recv()
@@ -202,14 +210,14 @@
         reply_out[half] = to_blocks(picked[:, 0:128], picked[:, 128:256], 128)
 
         def answer(step, carry, half=half):
-            rank = rem(me + step, 64)
+            rank, device = member(step, x, y, c, a, b)
             send(
                 reply_out.at[half, rank], replies.at[half, me],
-                reply_send.at[half], reply_recv.at[half], member(rank, a),
+                reply_send.at[half], reply_recv.at[half], device,
             )
             return carry
 
-        lax.fori_loop(1, 64, answer, 0)
+        lax.fori_loop(0, 63, answer, 0)
         replies[half, pl.ds(me, 1)] = reply_out[half, pl.ds(me, 1)]
 
     loads[2].wait()
@@ -297,11 +305,11 @@
     rows_out[...] = to_blocks(given[:, 0:256], given[:, 256:512], 256)
 
     def give_rows(step, carry):
-        rank = rem(me + step, 64)
-        send(rows_out.at[rank], rows_in.at[me], rows_send, rows_recv, member(rank, a))
+        rank, device = member(step, x, y, c, a, b)
+        send(rows_out.at[rank], rows_in.at[me], rows_send, rows_recv, device)
         return carry
 
-    lax.fori_loop(1, 64, give_rows, 0)
+    lax.fori_loop(0, 63, give_rows, 0)
     rows_in[pl.ds(me, 1)] = rows_out[pl.ds(me, 1)]
 
     grad_o = dot(cot, gated, ((0,), (0,))).astype(BF16)
@@ -315,54 +323,60 @@
     for part in range(4):
         waiter(pair_in.at[part], pair_send.at[part], pair_recv.at[part], here).wait()
         mine = grads[part, pl.ds(c, 1)].reshape(320, 512).astype(F32)
-        plane_out[part] = (mine + pair_in[part].astype(F32)).astype(BF16)
+        both = (mine + pair_in[part].astype(F32)).astype(BF16)
+        x_out[part] = both[0:160]
+        for to in range(4):
+            y_out[to, part] = both[160:320, 128 * to : 128 * to + 128]
     for step in range(1, 4):
         to_x, to_y = rem(x + step, 4), rem(y + step, 4)
         send(
-            plane_out.at[to_x, pl.ds(0, 160)], x_in.at[x], plane_send.at[0], plane_recv.at[0],
+            x_out.at[to_x], x_in.at[x], plane_send.at[0], plane_recv.at[0],
             (to_x * 16 + z, narrow),
         )
         send(
-            plane_out.at[:, pl.ds(160, 160), pl.ds(pl.multiple_of(128 * to_y, 128), 128)], y_in.at[y],
+            y_out.at[to_y], y_in.at[y],
             plane_send.at[1], plane_recv.at[1], (wide, 2 * to_y + c),
         )
-    my_lanes = pl.ds(pl.multiple_of(128 * y, 128), 128)
-    x_in[pl.ds(x, 1)] = plane_out[pl.ds(x, 1), 0:160]
-    y_in[pl.ds(y, 1)] = plane_out[:, 160:320, my_lanes].reshape(1, 4, 160, 128)
+    x_in[pl.ds(x, 1)] = x_out[pl.ds(x, 1)]
+    y_in[pl.ds(y, 1)] = y_out[pl.ds(y, 1)]
 
     waiter(rows_in.at[most], rows_send, rows_recv, here).wait()
     arrived = rows_in[...].astype(F32)
     for half in range(2):
         sums[half] = dot(chosen[...], arrived[:, 8 * half : 8 * half + 8].reshape(512, 256).astype(BF16), ((0,), (0,)))
 
-    def pass_sums():
+    child = (hops == 7).astype(I32)
+    place = jnp.where(hops == 1, 0, 1) + 1 - outward
+
+    def give_pieces(piece, values):
+        chain_out[piece] = values.astype(BF16)
+
+        def give(step, carry):
+            to = rem(narrow + step, 8)
+            send(
+                chain_out.at[piece, pl.ds(pl.multiple_of(32 * to, 32), 32)], piece_in.at[piece, place],
+                chain_send.at[piece], piece_recv.at[piece], (x * 16 + my_z, to),
+            )
+            return carry
+
+        lax.fori_loop(0, 8, give, 0)
+
+    def own_sums(piece):
+        return sums[piece // 2, :, 128 * (piece % 2) : 128 * (piece % 2) + 128]
+
+    @pl.when(is_far)
+    def _():
         for piece in range(4):
-            mine = sums[piece // 2, :, 128 * (piece % 2) : 128 * (piece % 2) + 128]
-            chain_out[piece] = mine.astype(BF16)
-
-            @pl.when(passes_on)
-            def _(piece=piece, mine=mine):
-                waiter(chain_in.at[piece], chain_send.at[piece], chain_recv.at[piece], here).wait_recv()
-                chain_out[piece] = (mine + chain_in[piece].astype(F32)).astype(BF16)
-
-            @pl.when(hops > 1)
-            def _(piece=piece):
-                send(
-                    chain_out.at[piece], chain_in.at[piece],
-                    chain_send.at[piece], chain_recv.at[piece], on_line(parent),
-                )
-
-            @pl.when(hops == 1)
-            def _(piece=piece):
-                for to in range(8):
-                    send(
-                        chain_out.at[piece, pl.ds(32 * to, 32)], piece_in.at[piece, div(1 - outward, 2)],
-                        chain_send.at[piece], piece_recv.at[piece], (x * 16 + my_z, to),
-                    )
-
-    @pl.when(hops > 1)
-    def _():
-        pass_sums()
+            chain_out[piece] = own_sums(piece).astype(BF16)
+            send(
+                chain_out.at[piece], chain_in.at[piece, child],
+                chain_send.at[piece], chain_recv.at[piece], on_line(parent),
+            )
+
+    @pl.when(hops == 1)
+    def _():
+        for piece in range(4):
+            give_pieces(piece, own_sums(piece))
 
     three = pl.ds(0, 3)
 
@@ -373,23 +387,27 @@
         return total
 
     waiter(x_in.at[three], plane_send.at[0], plane_recv.at[0], here).wait()
-    x_mid[...] = add_up(x_in).astype(BF16)
+    total = add_up(x_in).astype(BF16)
+    for to in range(4):
+        x_mid[to] = total[:, 128 * to : 128 * to + 128]
     for step in range(1, 4):
         to_y = rem(y + step, 4)
         send(
-            x_mid.at[:, pl.ds(pl.multiple_of(128 * to_y, 128), 128)], xy_in.at[y],
+            x_mid.at[to_y], xy_in.at[y],
             plane_send.at[2], plane_recv.at[2], (wide, 2 * to_y + c),
         )
-    xy_in[pl.ds(y, 1)] = x_mid[:, my_lanes].reshape(1, 160, 128)
+    xy_in[pl.ds(y, 1)] = x_mid[pl.ds(y, 1)]
     waiter(y_in.at[three], plane_send.at[1], plane_recv.at[1], here).wait()
     y_mid[...] = add_up(y_in).astype(BF16)
     for step in range(1, 4):
         to_x = rem(x + step, 4)
         send(y_mid.at[to_x], yx_in.at[x], plane_send.at[3], plane_recv.at[3], (to_x * 16 + z, narrow))
     yx_in[pl.ds(x, 1)] = y_mid[pl.ds(x, 1)]
-    @pl.when(hops == 1)
-    def _():
-        pass_sums()
+    @pl.when(is_relay)
+    def _():
+        for piece in range(4):
+            waiter(chain_in.at[piece], chain_send.at[piece], chain_recv.at[piece], here).wait_recv()
+            give_pieces(piece, own_sums(piece) + add_up(chain_in.at[piece]))
 
     waiter(xy_in.at[three], plane_send.at[2], plane_recv.at[2], here).wait()
     waiter(yx_in.at[three], plane_send.at[3], plane_recv.at[3], here).wait()
@@ -461,12 +479,13 @@
 
         @pl.when(is_source)
         def _(piece=piece):
+            for step in range(4):
+                waiter(shard.at[piece], shard_send.at[piece], shard_recv.at[piece], here).wait_send()
+
+        @pl.when(is_relay)
+        def _(piece=piece):
             for step in range(2):
-                waiter(shard.at[piece], shard_send.at[piece], shard_recv.at[piece], here).wait_send()
-
-        @pl.when(passes_on)
-        def _(piece=piece):
-            waiter(shard.at[piece], pass_send.at[piece], shard_recv.at[piece], here).wait_send()
+                waiter(shard.at[piece], pass_send.at[piece], shard_recv.at[piece], here).wait_send()
 
         waiter(chain_out.at[piece], chain_send.at[piece], chain_recv.at[piece], here).wait_send()
 
@@ -499,16 +518,16 @@
         scratch_shapes=[
             held(1, 128, kind=I32), held(1, 128, kind=I32), held(1, 6, kind=I32),
             held(128, 512), held(512, 2048), held(512, 512),
-            held(4, 256, 128), held(64, 8, 128, kind=F32), held(64, 8, 128, kind=F32), held(512, 256),
+            held(4, 256, 128), held(4, 256, 128), held(64, 8, 128, kind=F32), held(64, 8, 128, kind=F32), held(512, 256),
             held(2, 64, 16, 128), held(2, 64, 16, 128),
             held(128, 2048, kind=F32), held(128, 2048), held(128, 2048, kind=F32), held(128, 2048),
             held(4, 2, 320, 512), held(64, 16, 256), held(64, 16, 256),
-            held(4, 320, 512), held(4, 320, 512),
-            held(4, 160, 512), held(4, 4, 160, 128), held(160, 512), held(4, 160, 128),
+            held(4, 320, 512), held(4, 160, 512), held(4, 4, 160, 128),
+            held(4, 160, 512), held(4, 4, 160, 128), held(4, 160, 128), held(4, 160, 128),
             held(4, 160, 128), held(4, 160, 128),
             held(8, 2, 32, 128), held(16, 32, 128),
-            held(2, 256, 256, kind=F32), held(4, 256, 128), held(4, 256, 128), held(4, 2, 32, 128), held(2, 32, 256),
-            dma((6,)), dma((4,)), dma((4,)), dma((4,)), dma, dma, dma((2,)), dma((2,)),
+            held(2, 256, 256, kind=F32), held(4, 2, 256, 128), held(4, 256, 128), held(4, 4, 32, 128), held(2, 32, 256),
+            dma((10,)), dma((4,)), dma((4,)), dma((4,)), dma, dma, dma((2,)), dma((2,)),
             dma, dma, dma((4,)), dma((4,)), dma((4,)), dma((4,)), dma, dma,
             dma((4,)), dma((4,)), dma((4,)), dma((2,)), dma((2,)), dma((2,)),
         ],

time: 88.6 us -> 83.5 us (0.942)
  Pallas kernels: 87.7 us -> 81.9 us
    pallas_call x1, Pallas kernels: 85.9 us -> 80.1 us  [on_device(): pl.pallas_call(layer_kernel, out_shape=(shape((2, 8, 32, 256), BF16), sha...]
where the time goes in v5:
time: 83.5 us; the launch traced here: 82.6 us
  Pallas kernels  81.9 us (98%)
    pallas_call x1, Pallas kernels, on_device(): pl.pallas_call(layer_kernel, out_shape=(shape((2, 8, 32, 256), BF16), sha...  80.1 us
    pallas_call x1, Pallas kernels, on_device(): pl.pallas_call(finish_kernel, out_shape=(shape((256, 512), F32), shape((3...  1.79 us

profile of v5, /device:TPU:1, one launch (start us, length us, event | category | flops | bytes accessed | tf_op | source)
XLA Modules:
  0.0 82.6 jit_solution(13988265520228858391)
XLA Ops:
  0.6 80.1 %layer.1 = (bf16[2,8,32,256]{3,2,1,0:T(8,128)(2,1)}, f32[40,64]{1,0:T(8,128)}) custom-call(s32[1,128]{1,0:T(1,128)} %bitcast.4, s32[1,128]{1,0:T(1,128)} %bitcast.5, s32[1,6]{1,0:T(1,128)} %lengths_hbm.1, bf16[256,512]{1,0:T(8,128)(2,1)} %table.1, bf16[128,512]{1,0:T(8,128)(2,1)} %cotangent_hbm.1, bf16[512,2048]{1,0:T(8,128)(2,1)} %w_uvqk_hbm.1, ...), custom_call_target="tpu_custom_call" | custom-call | tf_op jit(solution)/shard_map/layer/pallas_call | solution.py:513
  80.8 1.8 %finish.1 = (f32[256,512]{1,0:T(8,128)}, f32[32,64]{1,0:T(8,128)}, f32[8,64]{1,0:T(8,128)}) custom-call(bf16[2,8,32,256]{3,2,1,0:T(8,128)(2,1)} %get-tuple-element.8.shared, f32[40,64]{1,0:T(8,128)} %get-tuple-element.9.sums), custom_call_target="tpu_custom_call" | custom-call | tf_op jit(solution)/shard_map/finish/pallas_call | solution.py:538

commit v6 on v5

--- a/solution.py
+++ b/solution.py
@@ -108,9 +108,9 @@
 
 def layer_kernel(
     owner_hbm, row_hbm, lengths_hbm, table, cotangent_hbm, w_uvqk_hbm, w_out_hbm, shared, out_w,
-    owner, row, lengths, cotangent, w_uvqk, w_out, own_shard, shard, ask_out, asked, chosen, reply_out, replies,
-    pre, act, grad_act, grad_pre, grads, rows_out, rows_in, pair_in, x_out, y_out, x_in, y_in, x_mid, y_mid, xy_in, yx_in,
-    line_out, line_in, sums, chain_in, chain_out, piece_in, share,
+    owner, row, lengths, cotangent, w_uvqk, w_out, own_shard, shard, ask_out, asked, chosen, gathers, reply_out, replies,
+    slope, act, held_att, att_slope, grad_act, grad_pre, grads, rows_out, rows_in, pair_in, x_out, y_out, x_in, y_in, x_mid, y_mid, xy_in, yx_in,
+    line_out, line_in, sums, chain_in, chain_out, piece_in, share, held_w,
     load_sem, shard_send, shard_recv, pass_send, ask_send, ask_recv, reply_send, reply_recv,
     rows_send, rows_recv, pair_send, pair_recv, plane_send, plane_recv, line_send, line_recv,
     chain_send, chain_recv, piece_recv, share_send, share_recv, keep_sem,
@@ -128,6 +128,7 @@
     outward = jnp.where(away < 8, 1, -1)
     hops = jnp.where(away < 8, away, 16 - away)
     is_relay = hops == 3
+    passes_on = jnp.logical_or(hops == 3, hops == 5)
     is_far = hops > 3
     upper = div(z, 8)
     in_half = (upper == c).astype(I32)
@@ -145,13 +146,13 @@
         loads[-1].start()
 
     parent = jnp.where(hops > 3, my_z + 3 * outward, my_z)
-    signal(barrier, on_line(parent))
+    signal(barrier, on_line(jnp.where(hops > 3, z - 2 * outward, my_z)))
 
     def greet(step, carry):
         signal(barrier, member(step, x, y, c, a, b)[1])
         return carry
 
-    lax.fori_loop(0, 63, greet, 0)
+    lax.fori_loop(0, 63, greet, 0, unroll=7)
 
     loads[0].wait()
     loads[1].wait()
@@ -166,70 +167,69 @@
 
     for piece in range(4):
         loads[6 + piece].wait()
-    pl.semaphore_wait(barrier, 63 + 4 * is_source.astype(I32) + 2 * is_relay.astype(I32))
+    pl.semaphore_wait(barrier, 63 + 4 * is_source.astype(I32) + passes_on.astype(I32))
 
     @pl.when(is_source)
     def _():
-        for piece in range(4):
-            for step in (3, -3, 1, -1):
-                send(
-                    own_shard.at[piece], shard.at[piece],
-                    shard_send.at[piece], shard_recv.at[piece], on_line(z + step),
-                )
+        for steps in ((3, -3), (1, -1)):
+            for piece in range(4):
+                for step in steps:
+                    send(
+                        own_shard.at[piece], shard.at[piece],
+                        shard_send.at[piece], shard_recv.at[piece], on_line(z + step),
+                    )
 
     def ask(step, carry):
         rank, device = member(step, x, y, c, a, b)
         send(ask_out.at[rank], asked.at[me], ask_send, ask_recv, device)
         return carry
 
-    lax.fori_loop(0, 63, ask, 0)
+    lax.fori_loop(0, 63, ask, 0, unroll=7)
     asked[pl.ds(me, 1)] = ask_out[pl.ds(me, 1)]
     most = pl.ds(0, 63)
 
-    @pl.when(is_relay)
+    @pl.when(passes_on)
     def _():
         for piece in range(4):
             waiter(shard.at[piece], shard_send.at[piece], shard_recv.at[piece], here).wait_recv()
-            for step in (4, 2):
-                send(
-                    shard.at[piece], shard.at[piece],
-                    pass_send.at[piece], shard_recv.at[piece], on_line(z + outward * step),
-                )
+            send(
+                shard.at[piece], shard.at[piece],
+                pass_send.at[piece], shard_recv.at[piece], on_line(z + outward * 2),
+            )
 
     waiter(asked.at[most], ask_send, ask_recv, here).wait_recv()
     wanted = asked[...].reshape(512, 128).astype(I32)
     wanted = jnp.concatenate([wanted, wanted], axis=1)
     chosen[...] = onehot(wanted == iota((512, 256), 1) + 1)
+    @pl.when(jnp.logical_not(passes_on))
+    def _():
+        for piece in range(4):
+            waiter(shard.at[piece], shard_send.at[piece], shard_recv.at[piece], here).wait_recv()
+
+    first = dot(chosen[...], jnp.concatenate([shard[0], shard[1]], axis=1))
+    second = dot(chosen[...], jnp.concatenate([shard[2], shard[3]], axis=1))
+    reply_out[...] = to_blocks(first, second, 256)
+
+    def answer(step, carry):
+        rank, device = member(step, x, y, c, a, b)
+        send(reply_out.at[rank], replies.at[me], reply_send, reply_recv, device)
+        return carry
+
+    lax.fori_loop(0, 63, answer, 0)
+    replies[pl.ds(me, 1)] = reply_out[pl.ds(me, 1)]
+
+    none = jnp.zeros((64, 8, 256), F32)
+    hits = chosen[...].astype(F32).reshape(64, 8, 256)
     for half in range(2):
-        @pl.when(jnp.logical_not(is_relay))
-        def _(half=half):
-            for piece in (2 * half, 2 * half + 1):
-                waiter(shard.at[piece], shard_send.at[piece], shard_recv.at[piece], here).wait_recv()
-
-        picked = dot(chosen[...], jnp.concatenate([shard[2 * half], shard[2 * half + 1]], axis=1))
-        reply_out[half] = to_blocks(picked[:, 0:128], picked[:, 128:256], 128)
-
-        def answer(step, carry, half=half):
-            rank, device = member(step, x, y, c, a, b)
-            send(
-                reply_out.at[half, rank], replies.at[half, me],
-                reply_send.at[half], reply_recv.at[half], device,
-            )
-            return carry
-
-        lax.fori_loop(0, 63, answer, 0)
-        replies[half, pl.ds(me, 1)] = reply_out[half, pl.ds(me, 1)]
-
+        spread = jnp.concatenate([none, hits] if half else [hits, none], axis=1)
+        gathers[256 * half : 256 * half + 256] = spread.reshape(1024, 256).T.astype(BF16)
     loads[2].wait()
     weight = weights_of_pairs(lengths)
     spots = iota((128, 1024), 1)
     finds = (onehot(spots == slot_t), onehot(spots == slot_t + 8))
-    parts = []
-    for half in range(2):
-        waiter(replies.at[half, most], reply_send.at[half], reply_recv.at[half], here).wait_recv()
-        arrived = replies[half].reshape(1024, 128)
-        parts += [dot(finds[0], arrived), dot(finds[1], arrived)]
-    embedded = jnp.concatenate(parts, axis=1)
+    waiter(replies.at[most], reply_send, reply_recv, here).wait_recv()
+    arrived = replies[...].reshape(1024, 256)
+    embedded = jnp.concatenate([dot(finds[0], arrived), dot(finds[1], arrived)], axis=1)
     center = embedded - mean_rows(embedded)
     embed_scale = lax.rsqrt(mean_rows(center * center) + EPS)
     embed_norm = center * embed_scale
@@ -239,8 +239,9 @@
     for part in range(4):
         cols = pl.ds(512 * part, 512)
         value = dot(normed, w_uvqk[:, cols])
-        pre[:, cols] = value
-        act[:, cols] = (value * jax.nn.sigmoid(value)).astype(BF16)
+        gain = jax.nn.sigmoid(value)
+        act[:, cols] = (value * gain).astype(BF16)
+        slope[:, cols] = gain * (1.0 + value * (1.0 - gain))
 
     first_half = iota((128, 128), 1) < 64
     keep = (first_half, jnp.logical_not(first_half))
@@ -253,7 +254,10 @@
         both = jnp.zeros((128, 128), F32)
         for head in range(2):
             score = dot(jnp.where(keep[head], q, zero), k, ((1,), (1,))) * 0.125
-            attention = (score * jax.nn.sigmoid(score) * weight).astype(BF16)
+            gain = jax.nn.sigmoid(score)
+            attention = (score * gain * weight).astype(BF16)
+            held_att[2 * pair + head] = attention
+            att_slope[2 * pair + head] = weight * (gain * (1.0 + score * (1.0 - gain))) * 0.125
             both = both + dot(attention, jnp.where(keep[head], v, zero))
         mixed.append(both)
     mixture = jnp.concatenate(mixed, axis=1)
@@ -269,9 +273,7 @@
 
     def back(part, grad_normed):
         cols = pl.ds(512 * part, 512)
-        value = pre[:, cols]
-        gain = jax.nn.sigmoid(value)
-        grad_pre[:, cols] = (grad_act[:, cols] * (gain * (1.0 + value * (1.0 - gain)))).astype(BF16)
+        grad_pre[:, cols] = (grad_act[:, cols] * slope[:, cols]).astype(BF16)
         return grad_normed + dot(grad_pre[:, cols], w_uvqk[:, cols], ((1,), (1,)))
 
     grad_gated = dot(cot, w_out[...], ((1,), (1,)))
@@ -286,12 +288,9 @@
         grad_q, grad_k, grad_v = [jnp.zeros((128, 128), F32)] * 3
         for head in range(2):
             q_one, k_one, v_one, g_one = [jnp.where(keep[head], part, zero) for part in (q, k, v, g)]
-            score = dot(q_one, k, ((1,), (1,))) * 0.125
-            gain = jax.nn.sigmoid(score)
-            attention = (score * gain * weight).astype(BF16)
             grad_att = dot(g_one, v, ((1,), (1,)))
-            grad_score = (grad_att * weight * (gain * (1.0 + score * (1.0 - gain))) * 0.125).astype(BF16)
-            grad_v = grad_v + dot(attention, g_one, ((0,), (0,)))
+            grad_score = (grad_att * att_slope[2 * pair + head]).astype(BF16)
+            grad_v = grad_v + dot(held_att[2 * pair + head], g_one, ((0,), (0,)))
             grad_q = grad_q + dot(grad_score, k_one)
             grad_k = grad_k + dot(grad_score, q_one, ((0,), (0,)))
         grad_act[:, 512 + 128 * pair : 640 + 128 * pair] = grad_v
@@ -309,7 +308,7 @@
         send(rows_out.at[rank], rows_in.at[me], rows_send, rows_recv, device)
         return carry
 
-    lax.fori_loop(0, 63, give_rows, 0)
+    lax.fori_loop(0, 63, give_rows, 0, unroll=7)
     rows_in[pl.ds(me, 1)] = rows_out[pl.ds(me, 1)]
 
     grad_o = dot(cot, gated, ((0,), (0,))).astype(BF16)
@@ -341,9 +340,7 @@
     y_in[pl.ds(y, 1)] = y_out[pl.ds(y, 1)]
 
     waiter(rows_in.at[most], rows_send, rows_recv, here).wait()
-    arrived = rows_in[...].astype(F32)
-    for half in range(2):
-        sums[half] = dot(chosen[...], arrived[:, 8 * half : 8 * half + 8].reshape(512, 256).astype(BF16), ((0,), (0,)))
+    sums[...] = dot(gathers[...], rows_in[...].reshape(1024, 256)).reshape(2, 256, 256)
 
     child = (hops == 7).astype(I32)
     place = jnp.where(hops == 1, 0, 1) + 1 - outward
@@ -423,17 +420,18 @@
             line_out[step, core] = jnp.concatenate([packed, values[rest], jnp.zeros((8, 128), F32)], axis=0).astype(BF16)
 
     def give_line(step, carry):
-        to_z = 8 * c + step
+        place = rem(z + 4 + step, 8)
+        to_z = 8 * c + place
         for core in range(2):
             own = jnp.logical_and(to_z == z, c == core)
 
             @pl.when(jnp.logical_not(own))
             def _():
-                send(line_out.at[step, core], line_in.at[z], line_send, line_recv, (x * 16 + to_z, 2 * y + core))
+                send(line_out.at[place, core], line_in.at[z], line_send, line_recv, (x * 16 + to_z, 2 * y + core))
 
             @pl.when(own)
             def _():
-                line_in[pl.ds(z, 1)] = line_out[pl.ds(step, 1), core]
+                line_in[pl.ds(z, 1)] = line_out[pl.ds(place, 1), core]
 
         return carry
 
@@ -467,13 +465,14 @@
         waiter(line_in, line_send, line_recv, here).wait()
 
     total = add_up(line_in)
-    out_w[0:16] = total[0:16, 0:64]
-    out_w[16:32] = total[0:16, 64:128]
-    out_w[32:40] = total[16:24, 0:64]
+    held_w[0:16] = total[0:16, 0:64]
+    held_w[16:32] = total[0:16, 64:128]
+    held_w[32:40] = total[16:24, 0:64]
+    keeps.append(pltpu.make_async_copy(held_w, out_w, keep_sem.at[2]))
+    keeps[2].start()
 
     waiter(asked.at[most], ask_send, ask_recv, here).wait_send()
-    for half in range(2):
-        waiter(replies.at[half, most], reply_send.at[half], reply_recv.at[half], here).wait_send()
+    waiter(replies.at[most], reply_send, reply_recv, here).wait_send()
 
     for piece in range(4):
 
@@ -482,21 +481,20 @@
             for step in range(4):
                 waiter(shard.at[piece], shard_send.at[piece], shard_recv.at[piece], here).wait_send()
 
-        @pl.when(is_relay)
+        @pl.when(passes_on)
         def _(piece=piece):
-            for step in range(2):
-                waiter(shard.at[piece], pass_send.at[piece], shard_recv.at[piece], here).wait_send()
+            waiter(shard.at[piece], pass_send.at[piece], shard_recv.at[piece], here).wait_send()
 
         waiter(chain_out.at[piece], chain_send.at[piece], chain_recv.at[piece], here).wait_send()
 
     for half in range(2):
         waiter(shared.at[half, pl.ds(0, 7)], share_send.at[half], share_recv.at[half], here).wait()
         keeps[half].wait()
+    keeps[2].wait()
 
 
 def finish_kernel(shared, sums, out_table, out_u, out_o):
-    for half in range(2):
-        out_table[:, 256 * half : 256 * half + 256] = shared[half].reshape(256, 256).astype(F32)
+    out_table[...] = shared[...].reshape(256, 256).astype(F32)
     out_u[...] = sums[0:32]
     out_o[...] = sums[32:40]
 
@@ -514,22 +512,23 @@
         layer_kernel,
         out_shape=(shape((2, 8, 32, 256), BF16), shape((40, 64), F32)),
         in_specs=[anywhere] * 7,
-        out_specs=(anywhere, vmem),
+        out_specs=(anywhere, anywhere),
         scratch_shapes=[
             held(1, 128, kind=I32), held(1, 128, kind=I32), held(1, 6, kind=I32),
             held(128, 512), held(512, 2048), held(512, 512),
-            held(4, 256, 128), held(4, 256, 128), held(64, 8, 128, kind=F32), held(64, 8, 128, kind=F32), held(512, 256),
-            held(2, 64, 16, 128), held(2, 64, 16, 128),
-            held(128, 2048, kind=F32), held(128, 2048), held(128, 2048, kind=F32), held(128, 2048),
+            held(4, 256, 128), held(4, 256, 128), held(64, 8, 128, kind=F32), held(64, 8, 128, kind=F32), held(512, 256), held(512, 1024),
+            held(64, 16, 256), held(64, 16, 256),
+            held(128, 2048, kind=F32), held(128, 2048), held(8, 128, 128), held(8, 128, 128, kind=F32),
+            held(128, 2048, kind=F32), held(128, 2048),
             held(4, 2, 320, 512), held(64, 16, 256), held(64, 16, 256),
             held(4, 320, 512), held(4, 160, 512), held(4, 4, 160, 128),
             held(4, 160, 512), held(4, 4, 160, 128), held(4, 160, 128), held(4, 160, 128),
             held(4, 160, 128), held(4, 160, 128),
             held(8, 2, 32, 128), held(16, 32, 128),
-            held(2, 256, 256, kind=F32), held(4, 2, 256, 128), held(4, 256, 128), held(4, 4, 32, 128), held(2, 32, 256),
-            dma((10,)), dma((4,)), dma((4,)), dma((4,)), dma, dma, dma((2,)), dma((2,)),
+            held(2, 256, 256, kind=F32), held(4, 2, 256, 128), held(4, 256, 128), held(4, 4, 32, 128), held(2, 32, 256), held(40, 64, kind=F32),
+            dma((10,)), dma((4,)), dma((4,)), dma((4,)), dma, dma, dma, dma,
             dma, dma, dma((4,)), dma((4,)), dma((4,)), dma((4,)), dma, dma,
-            dma((4,)), dma((4,)), dma((4,)), dma((2,)), dma((2,)), dma((2,)),
+            dma((4,)), dma((4,)), dma((4,)), dma((2,)), dma((2,)), dma((3,)),
         ],
         compiler_params=pltpu.CompilerParams(collective_id=0, has_side_effects=True, vmem_limit_bytes=VMEM_LIMIT),
         name="layer",
@@ -538,8 +537,16 @@
     grad_table, grad_uvqk, grad_out = pl.pallas_call(
         finish_kernel,
         out_shape=(shape((256, 512), F32), shape((32, 64), F32), shape((8, 64), F32)),
-        in_specs=[vmem] * 2,
-        out_specs=(vmem,) * 3,
+        grid=(2,),
+        in_specs=[
+            pl.BlockSpec((1, 8, 32, 256), lambda half: (half, 0, 0, 0)),
+            pl.BlockSpec((40, 64), lambda half: (0, 0)),
+        ],
+        out_specs=(
+            pl.BlockSpec((256, 256), lambda half: (0, half)),
+            pl.BlockSpec((32, 64), lambda half: (0, 0)),
+            pl.BlockSpec((8, 64), lambda half: (0, 0)),
+        ),
         name="finish",
     )(shared, sums)
     return grad_table, grad_uvqk.T, grad_out.T

time: 83.5 us -> 81.6 us (0.977); the launches traced: 82.6 us -> 81.5 us
  Pallas kernels: 81.9 us -> 80.9 us
    pallas_call x1, Pallas kernels: 80.1 us -> 79.1 us  [on_device(): pl.pallas_call(layer_kernel, out_shape=(shape((2, 8, 32, 256), BF16), sha...]
where the time goes in v6:
time: 81.6 us; the launch traced here: 81.5 us
  Pallas kernels  80.9 us (99%)
    pallas_call x1, Pallas kernels, on_device(): pl.pallas_call(layer_kernel, out_shape=(shape((2, 8, 32, 256), BF16), sha...  79.1 us
    pallas_call x1, Pallas kernels, on_device(): pl.pallas_call(finish_kernel, out_shape=(shape((256, 512), F32), shape((3...  1.74 us

profile of v6, /device:TPU:1, one launch (start us, length us, event | category | flops | bytes accessed | tf_op | source)
XLA Modules:
  0.0 81.5 jit_solution(6186446012754851352)
XLA Ops:
  0.6 79.1 %layer.1 = (bf16[2,8,32,256]{3,2,1,0:T(8,128)(2,1)}, f32[40,64]{1,0:T(8,128)}) custom-call(s32[1,128]{1,0:T(1,128)} %bitcast.4, s32[1,128]{1,0:T(1,128)} %bitcast.5, s32[1,6]{1,0:T(1,128)} %lengths_hbm.1, bf16[256,512]{1,0:T(8,128)(2,1)} %table.1, bf16[128,512]{1,0:T(8,128)(2,1)} %cotangent_hbm.1, bf16[512,2048]{1,0:T(8,128)(2,1)} %w_uvqk_hbm.1, ...), custom_call_target="tpu_custom_call" | custom-call | tf_op jit(solution)/shard_map/layer/pallas_call | solution.py:511
  79.8 1.7 %finish.1 = (f32[256,512]{1,0:T(8,128)}, f32[32,64]{1,0:T(8,128)}, f32[8,64]{1,0:T(8,128)}) custom-call(bf16[2,8,32,256]{3,2,1,0:T(8,128)(2,1)} %get-tuple-element.8.shared, f32[40,64]{1,0:T(8,128)} %get-tuple-element.9.sums), custom_call_target="tpu_custom_call" | custom-call | tf_op jit(solution)/shard_map/finish/pallas_call | solution.py:537

commit v7 on v6

--- a/solution.py
+++ b/solution.py
@@ -38,6 +38,16 @@
 
 def member(step, x, y, c, a, b):
     far = (div(step, 16), rem(div(step, 4), 4))
+    dx, dy = [jnp.where(i == 0, 2, jnp.where(i == 1, 1, jnp.where(i == 2, 3, 0))) for i in far]
+    to_x, to_y = rem(x + dx, 4), rem(y + dy, 4)
+    to_b, to_c = rem(b + 1 + rem(div(step, 2), 2), 2), rem(c + 1 + rem(step, 2), 2)
+    return to_x * 16 + shard_z(to_y, to_c, to_b), (to_x * 16 + 2 * a + to_b, 2 * to_y + to_c)
+
+
+def mixed_member(step, x, y, c, a, b):
+    chip = div(step, 4)
+    place = jnp.where(chip < 3, chip, jnp.where(chip < 15, chip + 1, 3))
+    far = (rem(rem(place, 4) + div(place, 4), 4), rem(place, 4))
     dx, dy = [jnp.where(i == 0, 2, jnp.where(i == 1, 1, jnp.where(i == 2, 3, 0))) for i in far]
     to_x, to_y = rem(x + dx, 4), rem(y + dy, 4)
     to_b, to_c = rem(b + 1 + rem(div(step, 2), 2), 2), rem(c + 1 + rem(step, 2), 2)
@@ -211,7 +221,7 @@
     reply_out[...] = to_blocks(first, second, 256)
 
     def answer(step, carry):
-        rank, device = member(step, x, y, c, a, b)
+        rank, device = mixed_member(step, x, y, c, a, b)
         send(reply_out.at[rank], replies.at[me], reply_send, reply_recv, device)
         return carry
 
@@ -304,7 +314,7 @@
     rows_out[...] = to_blocks(given[:, 0:256], given[:, 256:512], 256)
 
     def give_rows(step, carry):
-        rank, device = member(step, x, y, c, a, b)
+        rank, device = mixed_member(step, x, y, c, a, b)
         send(rows_out.at[rank], rows_in.at[me], rows_send, rows_recv, device)
         return carry
 
@@ -321,8 +331,7 @@
         send(grads.at[part, 1 - c], pair_in.at[part], pair_send.at[part], pair_recv.at[part], partner)
     for part in range(4):
         waiter(pair_in.at[part], pair_send.at[part], pair_recv.at[part], here).wait()
-        mine = grads[part, pl.ds(c, 1)].reshape(320, 512).astype(F32)
-        both = (mine + pair_in[part].astype(F32)).astype(BF16)
+        both = grads[part, pl.ds(c, 1)].reshape(320, 512) + pair_in[part]
         x_out[part] = both[0:160]
         for to in range(4):
             y_out[to, part] = both[160:320, 128 * to : 128 * to + 128]
@@ -420,7 +429,7 @@
             line_out[step, core] = jnp.concatenate([packed, values[rest], jnp.zeros((8, 128), F32)], axis=0).astype(BF16)
 
     def give_line(step, carry):
-        place = rem(z + 4 + step, 8)
+        place = rem(z + step + 4 * in_half, 8)
         to_z = 8 * c + place
         for core in range(2):
             own = jnp.logical_and(to_z == z, c == core)

time: 81.6 us -> 81.6 us (level)
  no operation moved by 1% of the time
where the time goes in v7:
time: 81.6 us; the launch traced here: 81.3 us
  Pallas kernels  80.7 us (99%)
    pallas_call x1, Pallas kernels, on_device(): pl.pallas_call(layer_kernel, out_shape=(shape((2, 8, 32, 256), BF16), sha...  78.9 us
    pallas_call x1, Pallas kernels, on_device(): pl.pallas_call(finish_kernel, out_shape=(shape((256, 512), F32), shape((3...  1.74 us

profile of v7, /device:TPU:1, one launch (start us, length us, event | category | flops | bytes accessed | tf_op | source)
XLA Modules:
  0.0 81.3 jit_solution(6372454149192868266)
XLA Ops:
  0.6 78.9 %layer.1 = (bf16[2,8,32,256]{3,2,1,0:T(8,128)(2,1)}, f32[40,64]{1,0:T(8,128)}) custom-call(s32[1,128]{1,0:T(1,128)} %bitcast.4, s32[1,128]{1,0:T(1,128)} %bitcast.5, s32[1,6]{1,0:T(1,128)} %lengths_hbm.1, bf16[256,512]{1,0:T(8,128)(2,1)} %table.1, bf16[128,512]{1,0:T(8,128)(2,1)} %cotangent_hbm.1, bf16[512,2048]{1,0:T(8,128)(2,1)} %w_uvqk_hbm.1, ...), custom_call_target="tpu_custom_call" | custom-call | tf_op jit(solution)/shard_map/layer/pallas_call | solution.py:520
  79.6 1.7 %finish.1 = (f32[256,512]{1,0:T(8,128)}, f32[32,64]{1,0:T(8,128)}, f32[8,64]{1,0:T(8,128)}) custom-call(bf16[2,8,32,256]{3,2,1,0:T(8,128)(2,1)} %get-tuple-element.8.shared, f32[40,64]{1,0:T(8,128)} %get-tuple-element.9.sums), custom_call_target="tpu_custom_call" | custom-call | tf_op jit(solution)/shard_map/finish/pallas_call | solution.py:546
